TPU v7x, 512 devices: a whole 4x8x8 slice. The times are simulated.
512 devices in a mesh: pairs: 32 (over z, y_lo), rows: 16 (over x, y_hi, core).
Axes of the slice: x: 4, y: 8 (y_hi: 2, y_lo: 4; y = y_hi * 4 + y_lo), z: 8, core: 2. Of those that a mesh axis runs over, the one named last changes fastest.
Arguments:
- matrix: float32 [32768, 8192], P('rows', 'pairs'), may hold values from -9 to 9
Outputs:
- rotated: float32 [32768, 8192], P('rows', 'pairs')
- rotated_gram: float32 [8192, 256], P('pairs')
All inputs are finite; a program needn't handle non-finite values.
Results may differ from a plain program's by a relative error of at most 0.0003.
Values sent between devices are 32-bit elements; how exact they have to be, the bound alone decides.
No kernel may reach another device: no remote copies, remote signals or barrier semaphores. Data moves between devices by JAX's collectives and lax.ppermute only.
A program may use at most 64 MiB of HBM per device.

v0:
```python
import jax
import jax.numpy as jnp
from jax import lax
from jax.sharding import PartitionSpec as P

ITERS = 3
STEPS = 2


highest = lax.Precision.HIGHEST


def passed_along(block, axis, distance):
    devices = range(lax.axis_size(axis))
    route = [(i - distance, i) for i in devices if i - distance in devices]
    return lax.ppermute(block, axis, route)


def right_solve(factor, values):
    return lax.linalg.triangular_solve(
        factor, values, left_side=False, lower=True, transpose_a=True
    )


def eigen_steps(gram_matrix):
    rotation = jnp.eye(gram_matrix.shape[0], dtype=jnp.float32)
    for sweep_index in range(ITERS):
        square = jnp.dot(
            gram_matrix, gram_matrix, precision=highest, preferred_element_type=jnp.float32
        )
        factor = jnp.linalg.cholesky(square)
        rotation = right_solve(
            factor,
            jnp.dot(rotation, gram_matrix, precision=highest, preferred_element_type=jnp.float32),
        )
        gram_matrix = right_solve(
            factor,
            jnp.dot(factor.T, gram_matrix, precision=highest, preferred_element_type=jnp.float32),
        )
        gram_matrix = 0.5 * (gram_matrix + gram_matrix.T)
    return (rotation, gram_matrix)


def block_inner(first, second):
    return lax.dot_general(
        first,
        second,
        (((0,), (0,)), ((), ())),
        precision=highest,
        preferred_element_type=jnp.float32,
    )


def pair_gram(leading, trailing, rows_all):
    paired = jnp.concatenate([leading, trailing], 1)
    summed_gram = lax.psum(block_inner(paired, paired), "rows")
    return summed_gram / rows_all


def per_device(matrix):
    seat_index = lax.axis_index("pairs")
    seat_count = lax.axis_size("pairs")
    block_width = matrix.shape[1] // 2
    rows_all = matrix.shape[0] * lax.axis_size("rows")
    leading = matrix[:, :block_width]
    trailing = matrix[:, block_width:]
    first_seat = seat_index == 0
    last_seat = seat_index == seat_count - 1
    for step_index in range(STEPS):
        if step_index > 0:
            outgoing = jnp.where(first_seat, trailing, leading)
            arrived = passed_along(outgoing, "pairs", 1)
            from_right = passed_along(trailing, "pairs", -1)
            new_leading = jnp.where(first_seat, leading, arrived)
            trailing = jnp.where(last_seat, leading, from_right)
            leading = new_leading
        gram_matrix = pair_gram(leading, trailing, rows_all)
        rotation, gram_matrix = eigen_steps(gram_matrix)
        paired = jnp.concatenate([leading, trailing], 1)
        paired = jnp.dot(paired, rotation, precision=highest, preferred_element_type=jnp.float32)
        leading = paired[:, :block_width]
        trailing = paired[:, block_width:]
    return (paired, gram_matrix)


def solution(mesh):
    return jax.shard_map(
        per_device,
        mesh=mesh,
        in_specs=(P("rows", "pairs"),),
        out_specs=(P("rows", "pairs"), P("pairs", None)),
        check_vma=False,
    )
```

profile of v0, /device:TPU:504, one launch (start us, length us, event | category | flops | bytes accessed | tf_op | source)
XLA Modules:
  0.0 945.3 jit_solution(9337960056010186737)
XLA Ops:
  13.5 175.3 %all-reduce.4.cloned.1.call-done = f32[256,256]{1,0:T(8,128)} async-done(((f32[256,256]{1,0:T(8,128)}), f32[256,256]{1,0:T(8,128)}) %all-reduce.4.cloned.1.call-update) | async-done | bytes 262160 | tf_op jit(solution)/shard_map/psum | solution.py:56
  190.5 11.7 %cholesky.298 = f32[128,128]{1,0:T(8,128)S(1)} custom-call(f32[128,128]{1,0:T(8,128)S(1)} %cholesky.498), custom_call_target="Cholesky" | custom-call | tf_op jit(solution)/shard_map/jit(cholesky)/cholesky | solution.py:31
  212.5 11.7 %cholesky.315 = f32[128,128]{1,0:T(8,128)S(1)} custom-call(f32[128,128]{1,0:T(8,128)S(1)} %convolution_subtract_fusion.16), custom_call_target="Cholesky" | custom-call | tf_op jit(solution)/shard_map/jit(cholesky)/cholesky | solution.py:31
  230.3 19.8 %custom-call.27 = f32[2,128,128]{1,2,0:T(8,128)S(1)} custom-call(f32[2,128,128]{2,1,0:T(8,128)S(1)} %get-tuple-element.72), custom_call_target="InvertDiagBlocksLowerTriangular" | custom-call | tf_op jit(solution)/shard_map/triangular_solve/custom-call.0 | solution.py:20
  253.4 11.7 %cholesky.332 = f32[128,128]{1,0:T(8,128)S(1)} custom-call(f32[128,128]{1,0:T(8,128)S(1)} %cholesky.501), custom_call_target="Cholesky" | custom-call | tf_op jit(solution)/shard_map/jit(cholesky)/cholesky | solution.py:31
  277.2 11.9 %cholesky.349 = f32[128,128]{1,0:T(8,128)S(1)} custom-call(f32[128,128]{1,0:T(8,128)S(1)} %convolution_subtract_fusion.15), custom_call_target="Cholesky" | custom-call | tf_op jit(solution)/shard_map/jit(cholesky)/cholesky | solution.py:31
  297.0 19.7 %custom-call.29 = f32[2,128,128]{1,2,0:T(8,128)S(1)} custom-call(f32[2,128,128]{2,1,0:T(8,128)S(1)} %get-tuple-element.73), custom_call_target="InvertDiagBlocksLowerTriangular" | custom-call | tf_op jit(solution)/shard_map/triangular_solve/custom-call.0 | solution.py:20
  327.2 11.7 %cholesky.366 = f32[128,128]{1,0:T(8,128)S(1)} custom-call(f32[128,128]{1,0:T(8,128)S(1)} %cholesky.504), custom_call_target="Cholesky" | custom-call | tf_op jit(solution)/shard_map/jit(cholesky)/cholesky | solution.py:31
  341.0 11.3 %custom-call.30 = f32[1,128,128]{1,2,0:T(8,128)} custom-call(f32[1,128,128]{2,1,0:T(8,128)} %get-tuple-element.164), custom_call_target="InvertDiagBlocksLowerTriangular" | custom-call | tf_op jit(solution)/shard_map/jit(cholesky)/cholesky | solution.py:31
  355.1 13.2 %cholesky.383 = f32[128,128]{1,0:T(8,128)} custom-call(f32[128,128]{1,0:T(8,128)} %convolution_subtract_fusion.14), custom_call_target="Cholesky" | custom-call | tf_op jit(solution)/shard_map/jit(cholesky)/cholesky | solution.py:31
  378.1 20.7 %custom-call.33 = f32[2,128,128]{1,2,0:T(8,128)} custom-call(f32[2,128,128]{2,1,0:T(8,128)S(1)} %get-tuple-element.76), custom_call_target="InvertDiagBlocksLowerTriangular" | custom-call | tf_op jit(solution)/shard_map/triangular_solve/custom-call.0 | solution.py:20
  418.3 17.9 %collective-permute-done = f32[2048,128]{0,1:T(8,128)} collective-permute-done((f32[2048,128]{0,1:T(8,128)}, f32[2048,128]{0,1:T(8,128)}, u32[]{:S(2)}, u32[]{:S(2)}) %collective-permute-start) | collective-permute-done | bytes 1048608 | tf_op jit(solution)/shard_map/ppermute | solution.py:16
  442.3 202.4 %all-reduce.6.cloned.1.call-done = f32[256,256]{1,0:T(8,128)} async-done(((f32[256,256]{1,0:T(8,128)}), f32[256,256]{1,0:T(8,128)}) %all-reduce.6.cloned.1.call-update) | async-done | bytes 262160 | tf_op jit(solution)/shard_map/psum | solution.py:56
  648.6 11.7 %cholesky.400 = f32[128,128]{1,0:T(8,128)S(1)} custom-call(f32[128,128]{1,0:T(8,128)S(1)} %cholesky.507), custom_call_target="Cholesky" | custom-call | tf_op jit(solution)/shard_map/jit(cholesky)/cholesky | solution.py:31
  672.4 12.1 %cholesky.417 = f32[128,128]{1,0:T(8,128)S(1)} custom-call(f32[128,128]{1,0:T(8,128)S(1)} %convolution_subtract_fusion.13), custom_call_target="Cholesky" | custom-call | tf_op jit(solution)/shard_map/jit(cholesky)/cholesky | solution.py:31
  694.1 20.5 %custom-call.35 = f32[2,128,128]{1,2,0:T(8,128)S(1)} custom-call(f32[2,128,128]{2,1,0:T(8,128)} %copy-done.30), custom_call_target="InvertDiagBlocksLowerTriangular" | custom-call | tf_op jit(solution)/shard_map/triangular_solve/custom-call.0 | solution.py:20
  728.5 13.2 %cholesky.434 = f32[128,128]{1,0:T(8,128)} custom-call(f32[128,128]{1,0:T(8,128)} %cholesky.510), custom_call_target="Cholesky" | custom-call | tf_op jit(solution)/shard_map/jit(cholesky)/cholesky | solution.py:31
  744.7 11.3 %custom-call.36 = f32[1,128,128]{1,2,0:T(8,128)} custom-call(f32[1,128,128]{2,1,0:T(8,128)} %get-tuple-element.156), custom_call_target="InvertDiagBlocksLowerTriangular" | custom-call | tf_op jit(solution)/shard_map/jit(cholesky)/cholesky | solution.py:31
  759.4 13.3 %cholesky.451 = f32[128,128]{1,0:T(8,128)} custom-call(f32[128,128]{1,0:T(8,128)} %convolution_subtract_fusion.12), custom_call_target="Cholesky" | custom-call | tf_op jit(solution)/shard_map/jit(cholesky)/cholesky | solution.py:31
  788.0 21.1 %custom-call.37 = f32[2,128,128]{1,2,0:T(8,128)} custom-call(f32[2,128,128]{2,1,0:T(8,128)} %get-tuple-element.78), custom_call_target="InvertDiagBlocksLowerTriangular" | custom-call | tf_op jit(solution)/shard_map/triangular_solve/custom-call.0 | solution.py:20
  826.7 13.2 %cholesky.468 = f32[128,128]{1,0:T(8,128)} custom-call(f32[128,128]{1,0:T(8,128)} %cholesky.513), custom_call_target="Cholesky" | custom-call | tf_op jit(solution)/shard_map/jit(cholesky)/cholesky | solution.py:31
  842.9 11.3 %custom-call.38 = f32[1,128,128]{1,2,0:T(8,128)} custom-call(f32[1,128,128]{2,1,0:T(8,128)} %get-tuple-element.152), custom_call_target="InvertDiagBlocksLowerTriangular" | custom-call | tf_op jit(solution)/shard_map/jit(cholesky)/cholesky | solution.py:31
  857.6 13.2 %cholesky.485 = f32[128,128]{1,0:T(8,128)} custom-call(f32[128,128]{1,0:T(8,128)} %convolution_subtract_fusion.11), custom_call_target="Cholesky" | custom-call | tf_op jit(solution)/shard_map/jit(cholesky)/cholesky | solution.py:31
  886.9 21.1 %custom-call.41 = f32[2,128,128]{1,2,0:T(8,128)} custom-call(f32[2,128,128]{2,1,0:T(8,128)} %get-tuple-element.81), custom_call_target="InvertDiagBlocksLowerTriangular" | custom-call | tf_op jit(solution)/shard_map/triangular_solve/custom-call.0 | solution.py:20
  (259 shorter events, 254.5 us)
Async XLA Ops:
  7.2 1.6 copy-start
  7.2 181.6 %all-reduce.4.cloned.1.call-start = ((), (), s32[]{:S(2)}) async-start(), calls=%async_computation | async-start | bytes 524288 | tf_op jit(solution)/shard_map/psum | solution.py:56
  13.0 631.7 %all-reduce.6.cloned.1.call-start = ((), (), s32[]{:S(2)}) async-start(), calls=%async_computation.1 | async-start | bytes 524288 | tf_op jit(solution)/shard_map/psum | solution.py:56
  190.2 60.0 %copy-start.9 = (f32[256,256]{1,0:T(8,128)S(1)}, f32[256,256]{1,0:T(8,128)}, u32[]{:S(2)}) copy-start(f32[256,256]{1,0:T(8,128)} %all-reduce.4.cloned.1.call-done) | copy-start | bytes 786436
  230.3 21.4 %copy-start.12 = (f32[256,256]{1,0:T(8,128)}, f32[256,256]{1,0:T(8,128)S(1)}, u32[]{:S(2)}) copy-start(f32[256,256]{1,0:T(8,128)S(1)} %get-tuple-element.456) | copy-start | bytes 786436
  250.2 1.7 copy-start.23
  297.0 24.2 %copy-start.13 = (f32[256,256]{1,0:T(8,128)}, f32[256,256]{1,0:T(8,128)S(1)}, u32[]{:S(2)}) copy-start(f32[256,256]{1,0:T(8,128)S(1)} %get-tuple-element.458) | copy-start | bytes 786436
  316.7 5.2 copy-start.25
  321.2 0.7 copy-start.10
  378.1 27.1 %copy-start.11 = (f32[256,128]{1,0:T(8,128)S(1)}, f32[256,128]{1,0:T(8,128)}, u32[]{:S(2)}) copy-start(f32[256,128]{1,0:T(8,128)} %copy-done.10) | copy-start | bytes 393220
  398.8 4.5 copy-start.26
  399.1 6.7 copy-start.29
  409.7 1.7 copy-start.1
  411.3 24.9 %collective-permute-start = (f32[2048,128]{0,1:T(8,128)}, f32[2048,128]{0,1:T(8,128)}, u32[]{:S(2)}, u32[]{:S(2)}) collective-permute-start(f32[2048,128]{0,1:T(8,128)} %get-tuple-element.147), channel_id=1, source_target_pairs={{0,16},{16,32},{32,48},{48,64},{64,80},{80,96},{96,112},{112,128},... | collective-permute-start | bytes 3145736 | tf_op jit(solution)/shard_map/ppermute | solution.py:16
  412.6 24.4 %collective-permute-start.1 = (f32[2048,128]{0,1:T(8,128)S(1)}, f32[2048,128]{0,1:T(8,128)}, u32[]{:S(2)}, u32[]{:S(2)}) collective-permute-start(f32[2048,128]{0,1:T(8,128)S(1)} %get-tuple-element.148), channel_id=1, source_target_pairs={{16,0},{32,16},{48,32},{64,48},{80,64},{96,80},{112,96},{128,112},... | collective-permute-start | bytes 3145736 | tf_op jit(solution)/shard_map/ppermute | solution.py:16
  438.8 1.0 copy-start.2
  714.6 5.0 copy-start.22
  825.3 0.7 copy-start.21
  922.4 6.6 copy-start.24
  922.4 8.4 copy-start.4
  922.4 8.4 copy-start.6
  922.4 8.5 copy-start.8
  923.7 7.7 copy-start.27
  927.3 6.0 copy-start.3
  (11 other events, 7.3 us)
Sparse Core Ops, SparseCore 0:
  13.1 175.6 all-reduce.3
  442.4 202.1 all-reduce.5
where the time goes:
time: 963 us; the launch traced here: 945 us
  waiting for transfers between devices  396 us (41%)
  other arithmetic  368 us (38%)
  matrix products  82.8 us (9%)
  local copies, waits for them, and re-layouts  67.1 us (7%)
  between operations  22.9 us (2%)
    psum x2, waiting for transfers between devices, pair_gram(): summed_gram = lax.psum(block_inner(paired, paired), 'rows')  378 us
    another operation x41, other arithmetic, eigen_steps(): factor = jnp.linalg.cholesky(square)  227 us
    another operation x18, other arithmetic, right_solve(): lax.linalg.triangular_solve(factor, values, left_side=False, lower=True,...  133 us
    another operation x52, local copies, waits for them, and re-layouts, right_solve(): lax.linalg.triangular_solve(factor, values, left_side=False, lower=True,...  43.7 us
    another operation x33, matrix products, right_solve(): lax.linalg.triangular_solve(factor, values, left_side=False, lower=True,...  32.1 us
  transfers between devices with their start and end apart: 4, of which 4 were waited for; matrix products, arithmetic and copies ran while one was open for 0% of the time, Pallas kernels for 0%

commit v1 on v0

v1 whole, which is shorter than its diff:
```python
import jax
import jax.numpy as jnp
from jax import lax
from jax.experimental import pallas as pl
from jax.experimental.pallas import tpu as pltpu
from jax.sharding import PartitionSpec as P

ITERS = 3
BLK = 128
SUB = 8
TILES = BLK // SUB
WIDE = 2

highest = lax.Precision.HIGHEST


def nn(a, b):
    return lax.dot_general(
        a, b, (((1,), (0,)), ((), ())), precision=highest, preferred_element_type=jnp.float32
    )


def tn(a, b):
    return lax.dot_general(
        a, b, (((0,), (0,)), ((), ())), precision=highest, preferred_element_type=jnp.float32
    )


def nt(a, b):
    return lax.dot_general(
        a, b, (((1,), (1,)), ((), ())), precision=highest, preferred_element_type=jnp.float32
    )


def lane(x, k):
    return jnp.broadcast_to(x[:, k : k + 1], (SUB, BLK))


def row(x, k):
    return jnp.broadcast_to(x[k : k + 1, :], (SUB, BLK))


def inverse_factor(square):
    lanes = lax.broadcasted_iota(jnp.int32, (SUB, BLK), 1)
    rows = lax.broadcasted_iota(jnp.int32, (SUB, BLK), 0)
    s = [square[SUB * q : SUB * q + SUB, :] for q in range(TILES)]
    w = [None] * TILES
    for p in range(0, TILES, WIDE):
        count = SUB * WIDE
        low = SUB * p
        inside = (lanes >= low) & (lanes < low + count)
        c = [[lane(s[p + r], low + k) for r in range(WIDE)] for k in range(count)]
        a = [
            jnp.where(inside, jnp.where(lanes == rows + SUB * (p + r), 1.0, 0.0), s[p + r])
            for r in range(WIDE)
        ]
        done = [None] * WIDE
        scale = [None] * WIDE
        for k in range(count):
            t, j = divmod(k, SUB)
            pivot = row(c[k][t], j)
            inv = 1.0 / pivot
            z = row(a[t], j)
            finished = z * lax.rsqrt(pivot)
            done[t] = finished if j == 0 else jnp.where(rows == j, finished, done[t])
            scale[t] = inv if j == 0 else jnp.where(rows == j, inv, scale[t])
            column = list(c[k])
            column[t] = jnp.where(rows == j, 0.0, column[t])
            factor = [column[r] * inv for r in range(WIDE)]
            for l in range(k + 1, count):
                m = row(c[l][t], j)
                for r in range(WIDE):
                    c[l][r] = c[l][r] - factor[r] * m
            for r in range(WIDE):
                a[r] = a[r] - factor[r] * z
        for r in range(WIDE):
            w[p + r] = jnp.where(lanes <= rows + SUB * (p + r), done[r], 0.0)
        if p + WIDE < TILES:
            y = [a[r] * scale[r] for r in range(WIDE)]
            ys = [row(y[k // SUB], k % SUB) for k in range(count)]
            for q in range(p + WIDE, TILES):
                o = [lane(s[q], low + k) for k in range(count)]
                even = o[0] * ys[0]
                odd = o[1] * ys[1]
                for k in range(2, count, 2):
                    even = even + o[k] * ys[k]
                    odd = odd + o[k + 1] * ys[k + 1]
                s[q] = jnp.where(inside, 0.0, s[q]) - (even + odd)
    return jnp.concatenate(w, 0)


def eigen_kernel(lead_ref, cross_ref, trail_ref, rotation_ref, gram_ref, g, z):
    g[:BLK, :BLK] = lead_ref[...]
    g[:BLK, BLK:] = cross_ref[...]
    g[BLK:, :BLK] = cross_ref[...].T
    g[BLK:, BLK:] = trail_ref[...]
    z[...] = g[...]

    def sweep(_, carry):
        za, zc = z[:, :BLK], z[:, BLK:]
        saa = tn(za, za)
        sac = tn(za, zc)
        scc = tn(zc, zc)
        wa = inverse_factor(saa)
        t = nn(wa, sac)
        va = nt(za, wa)
        xc = zc - nn(va, t)
        wc = inverse_factor(scc - tn(t, t))
        vc = nt(xc, wc)
        rotation_ref[:, :BLK] = va
        rotation_ref[:, BLK:] = vc
        z[...] = nn(g[...], rotation_ref[...])
        return carry

    lax.fori_loop(0, ITERS, sweep, 0)
    final = tn(rotation_ref[...], z[...])
    gram_ref[...] = 0.5 * (final + final.T)


def eigen_steps(lead, cross, trail):
    full = jax.ShapeDtypeStruct((2 * BLK, 2 * BLK), jnp.float32)
    vmem = pl.BlockSpec(memory_space=pltpu.VMEM)
    return pl.pallas_call(
        eigen_kernel,
        out_shape=(full, full),
        in_specs=[vmem] * 3,
        out_specs=(vmem, vmem),
        scratch_shapes=[pltpu.VMEM((2 * BLK, 2 * BLK), jnp.float32)] * 2,
        compiler_params=pltpu.CompilerParams(vmem_limit_bytes=32 * 1024 * 1024),
        name="eigen_steps",
    )(lead, cross, trail)


def swapped(x, bit):
    return lax.ppermute(x, "rows", [(i, i ^ bit) for i in range(lax.axis_size("rows"))])


def summed_over_rows(x, halve):
    if halve:
        odd = lax.axis_index("rows") % 2 == 1
        half = x.shape[0] // 2
        keep = jnp.where(odd, x[half:], x[:half])
        give = jnp.where(odd, x[:half], x[half:])
        part = keep + swapped(give, 1)
    else:
        part = x + swapped(x, 1)
    for bit in (4, 8, 2):
        part = part + swapped(part, bit)
    if halve:
        other = swapped(part, 1)
        return jnp.where(odd, jnp.concatenate([other, part], 0), jnp.concatenate([part, other], 0))
    return part


def moved(x, distance):
    devices = range(lax.axis_size("pairs"))
    return lax.ppermute(x, "pairs", [(i - distance, i) for i in devices if i - distance in devices])


def per_device(matrix):
    seat = lax.axis_index("pairs")
    first = seat == 0
    last = seat == lax.axis_size("pairs") - 1
    rows_all = matrix.shape[0] * lax.axis_size("rows")

    local = tn(matrix, matrix)
    packed = jnp.concatenate([local[:BLK, :BLK], local[:BLK, BLK:], local[BLK:, BLK:]], 0)
    packed = summed_over_rows(packed, True) / rows_all
    rotation, gram = eigen_steps(packed[:BLK], packed[BLK : 2 * BLK], packed[2 * BLK :])

    leading = nn(matrix, rotation[:, :BLK])
    trailing = nn(matrix, rotation[:, BLK:])
    lead_gram, trail_gram = gram[:BLK, :BLK], gram[BLK:, BLK:]

    arrived = moved(jnp.where(first, trailing, leading), 1)
    from_right = moved(trailing, -1)
    arrived_gram = moved(jnp.where(first, trail_gram, lead_gram), 1)
    from_right_gram = moved(trail_gram, -1)
    new_leading = jnp.where(first, leading, arrived)
    new_trailing = jnp.where(last, leading, from_right)
    new_lead_gram = jnp.where(first, lead_gram, arrived_gram)
    new_trail_gram = jnp.where(last, lead_gram, from_right_gram)

    cross = summed_over_rows(tn(new_leading, new_trailing), False) / rows_all
    rotation, gram = eigen_steps(new_lead_gram, cross, new_trail_gram)
    paired = nn(new_leading, rotation[:BLK]) + nn(new_trailing, rotation[BLK:])
    return paired, gram


def solution(mesh):
    return jax.shard_map(
        per_device,
        mesh=mesh,
        in_specs=(P("rows", "pairs"),),
        out_specs=(P("rows", "pairs"), P("pairs", None)),
        check_vma=False,
    )
```

time: 963 us -> 193 us (0.20)
  the two profiles are of different devices: /device:TPU:504 before, /device:TPU:248 now
where the time goes in v1:
time: 193 us; the launch traced here: 192 us
  waiting for transfers between devices  71 us (37%)
  starting transfers between devices  49.8 us (26%)
  Pallas kernels  49.2 us (25%)
  matrix products  19.6 us (10%)
    pallas_call x2, Pallas kernels, eigen_steps(): pl.pallas_call(eigen_kernel, out_shape=(full, full), in_specs=[vmem] * 3,...  49.2 us
    ppermute x4, waiting for transfers between devices, moved(): lax.ppermute(x, 'pairs', [(i - distance, i) for i in devices if i - dista...  44.3 us
    ppermute x9, starting transfers between devices, swapped(): lax.ppermute(x, 'rows', [(i, i ^ bit) for i in range(lax.axis_size('rows'...  30.1 us
    ppermute x9, waiting for transfers between devices, swapped(): lax.ppermute(x, 'rows', [(i, i ^ bit) for i in range(lax.axis_size('rows'...  26.6 us
    ppermute x4, starting transfers between devices, moved(): lax.ppermute(x, 'pairs', [(i - distance, i) for i in devices if i - dista...  19.7 us
    dot_general x4, matrix products, nn(): lax.dot_general(a, b, (((1,), (0,)), ((), ())), precision=highest, prefer...  13.5 us
    dot_general x2, matrix products, tn(): lax.dot_general(a, b, (((0,), (0,)), ((), ())), precision=highest, prefer...  6.08 us
  transfers between devices with their start and end apart: 13, of which 10 were waited for; matrix products, arithmetic and copies ran while one was open for 0% of the time, Pallas kernels for 0%

profile of v1, /device:TPU:248, one launch (start us, length us, event | category | flops | bytes accessed | tf_op | source)
XLA Modules:
  0.0 192.3 jit_solution(4474934981327843820)
XLA Ops:
  2.2 3.5 %fusion.9 = f32[256,256]{1,0:T(8,128)S(1)} fusion(f32[2048,256]{1,0:T(8,128)S(1)} %copy-done), kind=kOutput, calls=%fused_computation.23 | convolution fusion | flops 1610612736 | bytes 2359296 | tf_op jit(solution)/shard_map/dot_general | solution.py:24
  9.0 3.4 %collective-permute-start.1 = (f32[192,128]{1,0:T(8,128)S(1)}, f32[192,128]{1,0:T(8,128)S(1)}, u32[]{:S(2)}, u32[]{:S(2)}) collective-permute-start(f32[192,128]{1,0:T(8,128)S(1)} %select_add_fusion), channel_id=1, source_target_pairs={{0,4},{1,5},{2,6},{3,7},{4,0},{5,1},{6,2},{7,3},{8,12},{9,13},{10,... | collective-permute-start | bytes 294920 | tf_op jit(solution)/shard_map/ppermute | solution.py:135
  12.4 3.3 %collective-permute-done.1 = f32[192,128]{1,0:T(8,128)S(1)} collective-permute-done((f32[192,128]{1,0:T(8,128)S(1)}, f32[192,128]{1,0:T(8,128)S(1)}, u32[]{:S(2)}, u32[]{:S(2)}) %collective-permute-start.1) | collective-permute-done | bytes 98336 | tf_op jit(solution)/shard_map/ppermute | solution.py:135
  15.8 4.9 %collective-permute-start.2 = (f32[192,128]{1,0:T(8,128)S(1)}, f32[192,128]{1,0:T(8,128)S(1)}, u32[]{:S(2)}, u32[]{:S(2)}) collective-permute-start(f32[192,128]{1,0:T(8,128)S(1)} %add.33), channel_id=1, source_target_pairs={{0,8},{1,9},{2,10},{3,11},{4,12},{5,13},{6,14},{7,15},{8,0},{9,1},... | collective-permute-start | bytes 294920 | tf_op jit(solution)/shard_map/ppermute | solution.py:135
  20.7 3.1 %collective-permute-done.2 = f32[192,128]{1,0:T(8,128)S(1)} collective-permute-done((f32[192,128]{1,0:T(8,128)S(1)}, f32[192,128]{1,0:T(8,128)S(1)}, u32[]{:S(2)}, u32[]{:S(2)}) %collective-permute-start.2) | collective-permute-done | bytes 98336 | tf_op jit(solution)/shard_map/ppermute | solution.py:135
  23.8 4.7 %collective-permute-start.3 = (f32[192,128]{1,0:T(8,128)S(1)}, f32[192,128]{1,0:T(8,128)S(1)}, u32[]{:S(2)}, u32[]{:S(2)}) collective-permute-start(f32[192,128]{1,0:T(8,128)S(1)} %add.34), channel_id=1, source_target_pairs={{0,2},{1,3},{2,0},{3,1},{4,6},{5,7},{6,4},{7,5},{8,10},{9,11},{10,... | collective-permute-start | bytes 294920 | tf_op jit(solution)/shard_map/ppermute | solution.py:135
  28.5 6.7 %collective-permute-done.3 = f32[192,128]{1,0:T(8,128)S(1)} collective-permute-done((f32[192,128]{1,0:T(8,128)S(1)}, f32[192,128]{1,0:T(8,128)S(1)}, u32[]{:S(2)}, u32[]{:S(2)}) %collective-permute-start.3) | collective-permute-done | bytes 98336 | tf_op jit(solution)/shard_map/ppermute | solution.py:135
  38.5 24.2 %eigen_steps.2 = (f32[256,256]{1,0:T(8,128)S(1)}, f32[256,256]{1,0:T(8,128)S(1)}) custom-call(f32[128,128]{1,0:T(8,128)S(1)} %get-tuple-element.16.lead_ref, f32[128,128]{1,0:T(8,128)S(1)} %get-tuple-element.15.cross_ref, f32[128,128]{1,0:T(8,128)S(1)} %get-tuple-element.14.trail_ref), custom_call_target="tpu_custom_call" | custom-call | tf_op jit(solution)/shard_map/eigen_steps/pallas_call | solution.py:123
  62.8 2.3 %convolution_bitcast_fusion.1 = f32[2048,128]{0,1:T(8,128)S(1)} fusion(f32[2048,256]{1,0:T(8,128)S(1)} %copy-done, f32[256,256]{1,0:T(8,128)S(1)} %get-tuple-element.6), kind=kOutput, calls=%fused_computation.2 | convolution fusion | flops 805306368 | bytes 3276800 | tf_op jit(solution)/shard_map/dot_general | solution.py:18
  65.1 3.6 %broadcast_select_fusion.2 = (f32[2048,128]{0,1:T(8,128)}, f32[2048,128]{0,1:T(8,128)}) fusion(f32[2048,128]{0,1:T(8,128)S(1)} %convolution_bitcast_fusion.1, pred[]{:T(512)S(6)} %eq.11, f32[2048,256]{1,0:T(8,128)S(1)} %copy-done, f32[256,256]{1,0:T(8,128)S(1)} %get-tuple-element.6), kind=kOutput, calls=%fused_computation.5 | convolution fusion | flops 805568512 | bytes 5373953 | tf_op jit(solution)/shard_map/dot_general | solution.py:18
  68.8 7.8 %collective-permute-start.5 = (f32[2048,128]{0,1:T(8,128)}, f32[2048,128]{0,1:T(8,128)}, u32[]{:S(2)}, u32[]{:S(2)}) collective-permute-start(f32[2048,128]{0,1:T(8,128)} %get-tuple-element.17), channel_id=1, source_target_pairs={{0,16},{16,32},{32,48},{48,64},{64,80},{80,96},{96,112},{112,128},... | collective-permute-start | bytes 3145736 | tf_op jit(solution)/shard_map/ppermute | solution.py:157
  78.5 21.9 %collective-permute-done.5 = f32[2048,128]{0,1:T(8,128)} collective-permute-done((f32[2048,128]{0,1:T(8,128)}, f32[2048,128]{0,1:T(8,128)}, u32[]{:S(2)}, u32[]{:S(2)}) %collective-permute-start.5) | collective-permute-done | bytes 1048608 | tf_op jit(solution)/shard_map/ppermute | solution.py:157
  100.4 22.4 %collective-permute-done.7 = f32[2048,128]{0,1:T(8,128)} collective-permute-done((f32[2048,128]{0,1:T(8,128)}, f32[2048,128]{0,1:T(8,128)}, u32[]{:S(2)}, u32[]{:S(2)}) %collective-permute-start.7) | collective-permute-done | bytes 1048608 | tf_op jit(solution)/shard_map/ppermute | solution.py:157
  122.8 2.6 %fusion = f32[128,128]{1,0:T(8,128)S(1)} fusion(f32[2048,128]{0,1:T(8,128)S(1)} %convolution_bitcast_fusion.1, f32[2048,128]{0,1:T(8,128)} %collective-permute-done.5, pred[]{:T(512)S(6)} %eq.11, f32[2048,128]{0,1:T(8,128)} %collective-permute-done.7, pred[]{:T(512)S(6)} %eq.13), kind=kOutput, calls=%fused_computation.6 | convolution fusion | flops 403177472 | bytes 3211266 | tf_op jit(solution)/shard_map/dot_general | solution.py:24
  128.6 3.4 %collective-permute-start.9 = (f32[128,128]{1,0:T(8,128)S(1)}, f32[128,128]{1,0:T(8,128)S(1)}, u32[]{:S(2)}, u32[]{:S(2)}) collective-permute-start(f32[128,128]{1,0:T(8,128)S(1)} %add.36), channel_id=1, source_target_pairs={{0,4},{1,5},{2,6},{3,7},{4,0},{5,1},{6,2},{7,3},{8,12},{9,13},{10,... | collective-permute-start | bytes 196616 | tf_op jit(solution)/shard_map/ppermute | solution.py:135
  132.0 2.7 %collective-permute-done.9 = f32[128,128]{1,0:T(8,128)S(1)} collective-permute-done((f32[128,128]{1,0:T(8,128)S(1)}, f32[128,128]{1,0:T(8,128)S(1)}, u32[]{:S(2)}, u32[]{:S(2)}) %collective-permute-start.9) | collective-permute-done | bytes 65568 | tf_op jit(solution)/shard_map/ppermute | solution.py:135
  134.8 4.9 %collective-permute-start.10 = (f32[128,128]{1,0:T(8,128)S(1)}, f32[128,128]{1,0:T(8,128)S(1)}, u32[]{:S(2)}, u32[]{:S(2)}) collective-permute-start(f32[128,128]{1,0:T(8,128)S(1)} %add.37), channel_id=1, source_target_pairs={{0,8},{1,9},{2,10},{3,11},{4,12},{5,13},{6,14},{7,15},{8,0},{9,1},... | collective-permute-start | bytes 196616 | tf_op jit(solution)/shard_map/ppermute | solution.py:135
  139.7 3.9 %collective-permute-start.12 = (f32[128,128]{1,0:T(8,128)S(1)}, f32[128,128]{1,0:T(8,128)S(1)}, u32[]{:S(2)}, u32[]{:S(2)}) collective-permute-start(f32[128,128]{1,0:T(8,128)S(1)} %get-tuple-element.12), channel_id=1, source_target_pairs={{16,0},{32,16},{48,32},{64,48},{80,64},{96,80},{112,96},{128,112},... | collective-permute-start | bytes 196616 | tf_op jit(solution)/shard_map/ppermute | solution.py:157
  143.6 6.1 %collective-permute-start.6 = (f32[128,128]{1,0:T(8,128)S(1)}, f32[128,128]{1,0:T(8,128)S(1)}, u32[]{:S(2)}, u32[]{:S(2)}) collective-permute-start(f32[128,128]{1,0:T(8,128)S(1)} %get-tuple-element.13), channel_id=1, source_target_pairs={{0,16},{16,32},{32,48},{48,64},{64,80},{80,96},{96,112},{112,128},... | collective-permute-start | bytes 196616 | tf_op jit(solution)/shard_map/ppermute | solution.py:157
  149.7 2.8 %collective-permute-start.11 = (f32[128,128]{1,0:T(8,128)S(1)}, f32[128,128]{1,0:T(8,128)S(1)}, u32[]{:S(2)}, u32[]{:S(2)}) collective-permute-start(f32[128,128]{1,0:T(8,128)S(1)} %add.38), channel_id=1, source_target_pairs={{0,2},{1,3},{2,0},{3,1},{4,6},{5,7},{6,4},{7,5},{8,10},{9,11},{10,... | collective-permute-start | bytes 196616 | tf_op jit(solution)/shard_map/ppermute | solution.py:135
  152.6 7.2 %collective-permute-done.11 = f32[128,128]{1,0:T(8,128)S(1)} collective-permute-done((f32[128,128]{1,0:T(8,128)S(1)}, f32[128,128]{1,0:T(8,128)S(1)}, u32[]{:S(2)}, u32[]{:S(2)}) %collective-permute-start.11) | collective-permute-done | bytes 65568 | tf_op jit(solution)/shard_map/ppermute | solution.py:135
  159.8 25.0 %eigen_steps.3 = (f32[256,256]{1,0:T(8,128)S(1)}, f32[256,256]{1,0:T(8,128)}) custom-call(f32[128,128]{1,0:T(8,128)S(1)} %get-tuple-element.11.lead_ref, f32[128,128]{1,0:T(8,128)S(1)} %add_multiply_fusion.cross_ref, f32[128,128]{1,0:T(8,128)S(1)} %get-tuple-element.10.trail_ref), custom_call_target="tpu_custom_call" | custom-call | tf_op jit(solution)/shard_map/eigen_steps/pallas_call | solution.py:123
  184.8 3.1 %fusion.1 = f32[2048,256]{1,0:T(8,128)S(1)} fusion(f32[2048,128]{0,1:T(8,128)S(1)} %convolution_bitcast_fusion.1, f32[2048,128]{0,1:T(8,128)} %collective-permute-done.7, pred[]{:T(512)S(6)} %eq.13, f32[256,256]{1,0:T(8,128)S(1)} %get-tuple-element.8), kind=kOutput, calls=%fused_computation.7 | convolution fusion | flops 805568512 | bytes 4325377 | tf_op jit(solution)/shard_map/dot_general | solution.py:18
  187.9 4.4 %convolution_add_fusion = f32[2048,256]{1,0:T(8,128)} fusion(f32[2048,256]{1,0:T(8,128)S(1)} %fusion.1, f32[2048,128]{0,1:T(8,128)S(1)} %convolution_bitcast_fusion.1, f32[2048,128]{0,1:T(8,128)} %collective-permute-done.5, pred[]{:T(512)S(6)} %eq.11, f32[256,256]{1,0:T(8,128)S(1)} %get-tuple-element.8), kind=kOutput, calls=%fused_computation | convolution fusion | flops 806092800 | bytes 6422529 | tf_op jit(solution)/shard_map/dot_general | solution.py:18
  (27 shorter events, 13.2 us)
Async XLA Ops:
  0.6 1.6 copy-start
  5.8 3.2 %collective-permute-start = (f32[192,128]{1,0:T(8,128)S(1)}, f32[192,128]{1,0:T(8,128)S(1)}, u32[]{:S(2)}, u32[]{:S(2)}) collective-permute-start(f32[192,128]{1,0:T(8,128)S(1)} %slice_select_fusion), channel_id=1, source_target_pairs={{0,1},{1,0},{2,3},{3,2},{4,5},{5,4},{6,7},{7,6},{8,9},{9,8},{10,11... | collective-permute-start | bytes 294920 | tf_op jit(solution)/shard_map/ppermute | solution.py:135
  9.0 6.7 %collective-permute-start.1 = (f32[192,128]{1,0:T(8,128)S(1)}, f32[192,128]{1,0:T(8,128)S(1)}, u32[]{:S(2)}, u32[]{:S(2)}) collective-permute-start(f32[192,128]{1,0:T(8,128)S(1)} %select_add_fusion), channel_id=1, source_target_pairs={{0,4},{1,5},{2,6},{3,7},{4,0},{5,1},{6,2},{7,3},{8,12},{9,13},{10,... | collective-permute-start | bytes 294920 | tf_op jit(solution)/shard_map/ppermute | solution.py:135
  15.8 8.0 %collective-permute-start.2 = (f32[192,128]{1,0:T(8,128)S(1)}, f32[192,128]{1,0:T(8,128)S(1)}, u32[]{:S(2)}, u32[]{:S(2)}) collective-permute-start(f32[192,128]{1,0:T(8,128)S(1)} %add.33), channel_id=1, source_target_pairs={{0,8},{1,9},{2,10},{3,11},{4,12},{5,13},{6,14},{7,15},{8,0},{9,1},... | collective-permute-start | bytes 294920 | tf_op jit(solution)/shard_map/ppermute | solution.py:135
  23.8 11.5 %collective-permute-start.3 = (f32[192,128]{1,0:T(8,128)S(1)}, f32[192,128]{1,0:T(8,128)S(1)}, u32[]{:S(2)}, u32[]{:S(2)}) collective-permute-start(f32[192,128]{1,0:T(8,128)S(1)} %add.34), channel_id=1, source_target_pairs={{0,2},{1,3},{2,0},{3,1},{4,6},{5,7},{6,4},{7,5},{8,10},{9,11},{10,... | collective-permute-start | bytes 294920 | tf_op jit(solution)/shard_map/ppermute | solution.py:135
  35.3 3.2 %collective-permute-start.4 = (f32[192,128]{1,0:T(8,128)S(1)}, f32[192,128]{1,0:T(8,128)S(1)}, u32[]{:S(2)}, u32[]{:S(2)}) collective-permute-start(f32[192,128]{1,0:T(8,128)S(1)} %add.35), channel_id=1, source_target_pairs={{0,1},{1,0},{2,3},{3,2},{4,5},{5,4},{6,7},{7,6},{8,9},{9,8},{10,11... | collective-permute-start | bytes 294920 | tf_op jit(solution)/shard_map/ppermute | solution.py:135
  68.8 31.7 %collective-permute-start.5 = (f32[2048,128]{0,1:T(8,128)}, f32[2048,128]{0,1:T(8,128)}, u32[]{:S(2)}, u32[]{:S(2)}) collective-permute-start(f32[2048,128]{0,1:T(8,128)} %get-tuple-element.17), channel_id=1, source_target_pairs={{0,16},{16,32},{32,48},{48,64},{64,80},{80,96},{96,112},{112,128},... | collective-permute-start | bytes 3145736 | tf_op jit(solution)/shard_map/ppermute | solution.py:157
  76.6 46.3 %collective-permute-start.7 = (f32[2048,128]{0,1:T(8,128)}, f32[2048,128]{0,1:T(8,128)}, u32[]{:S(2)}, u32[]{:S(2)}) collective-permute-start(f32[2048,128]{0,1:T(8,128)} %get-tuple-element.18), channel_id=1, source_target_pairs={{16,0},{32,16},{48,32},{64,48},{80,64},{96,80},{112,96},{128,112},... | collective-permute-start | bytes 3145736 | tf_op jit(solution)/shard_map/ppermute | solution.py:157
  125.5 3.1 %collective-permute-start.8 = (f32[128,128]{1,0:T(8,128)S(1)}, f32[128,128]{1,0:T(8,128)S(1)}, u32[]{:S(2)}, u32[]{:S(2)}) collective-permute-start(f32[128,128]{1,0:T(8,128)S(1)} %fusion), channel_id=1, source_target_pairs={{0,1},{1,0},{2,3},{3,2},{4,5},{5,4},{6,7},{7,6},{8,9},{9,8},{10,11... | collective-permute-start | bytes 196616 | tf_op jit(solution)/shard_map/ppermute | solution.py:135
  128.6 6.2 %collective-permute-start.9 = (f32[128,128]{1,0:T(8,128)S(1)}, f32[128,128]{1,0:T(8,128)S(1)}, u32[]{:S(2)}, u32[]{:S(2)}) collective-permute-start(f32[128,128]{1,0:T(8,128)S(1)} %add.36), channel_id=1, source_target_pairs={{0,4},{1,5},{2,6},{3,7},{4,0},{5,1},{6,2},{7,3},{8,12},{9,13},{10,... | collective-permute-start | bytes 196616 | tf_op jit(solution)/shard_map/ppermute | solution.py:135
  134.8 14.9 %collective-permute-start.10 = (f32[128,128]{1,0:T(8,128)S(1)}, f32[128,128]{1,0:T(8,128)S(1)}, u32[]{:S(2)}, u32[]{:S(2)}) collective-permute-start(f32[128,128]{1,0:T(8,128)S(1)} %add.37), channel_id=1, source_target_pairs={{0,8},{1,9},{2,10},{3,11},{4,12},{5,13},{6,14},{7,15},{8,0},{9,1},... | collective-permute-start | bytes 196616 | tf_op jit(solution)/shard_map/ppermute | solution.py:135
  139.7 12.9 %collective-permute-start.12 = (f32[128,128]{1,0:T(8,128)S(1)}, f32[128,128]{1,0:T(8,128)S(1)}, u32[]{:S(2)}, u32[]{:S(2)}) collective-permute-start(f32[128,128]{1,0:T(8,128)S(1)} %get-tuple-element.12), channel_id=1, source_target_pairs={{16,0},{32,16},{48,32},{64,48},{80,64},{96,80},{112,96},{128,112},... | collective-permute-start | bytes 196616 | tf_op jit(solution)/shard_map/ppermute | solution.py:157
  143.6 9.0 %collective-permute-start.6 = (f32[128,128]{1,0:T(8,128)S(1)}, f32[128,128]{1,0:T(8,128)S(1)}, u32[]{:S(2)}, u32[]{:S(2)}) collective-permute-start(f32[128,128]{1,0:T(8,128)S(1)} %get-tuple-element.13), channel_id=1, source_target_pairs={{0,16},{16,32},{32,48},{48,64},{64,80},{80,96},{96,112},{112,128},... | collective-permute-start | bytes 196616 | tf_op jit(solution)/shard_map/ppermute | solution.py:157
  149.7 10.1 %collective-permute-start.11 = (f32[128,128]{1,0:T(8,128)S(1)}, f32[128,128]{1,0:T(8,128)S(1)}, u32[]{:S(2)}, u32[]{:S(2)}) collective-permute-start(f32[128,128]{1,0:T(8,128)S(1)} %add.38), channel_id=1, source_target_pairs={{0,2},{1,3},{2,0},{3,1},{4,6},{5,7},{6,4},{7,5},{8,10},{9,11},{10,... | collective-permute-start | bytes 196616 | tf_op jit(solution)/shard_map/ppermute | solution.py:135

commit v2 on v1

--- a/solution.py
+++ b/solution.py
@@ -10,6 +10,7 @@
 SUB = 8
 TILES = BLK // SUB
 WIDE = 2
+EARLY = 5
 
 highest = lax.Precision.HIGHEST
 
@@ -135,26 +136,38 @@
     return lax.ppermute(x, "rows", [(i, i ^ bit) for i in range(lax.axis_size("rows"))])
 
 
-def summed_over_rows(x, halve):
-    if halve:
-        odd = lax.axis_index("rows") % 2 == 1
-        half = x.shape[0] // 2
-        keep = jnp.where(odd, x[half:], x[:half])
-        give = jnp.where(odd, x[:half], x[half:])
-        part = keep + swapped(give, 1)
-    else:
-        part = x + swapped(x, 1)
-    for bit in (4, 8, 2):
-        part = part + swapped(part, bit)
-    if halve:
-        other = swapped(part, 1)
-        return jnp.where(odd, jnp.concatenate([other, part], 0), jnp.concatenate([part, other], 0))
-    return part
+def summed_over_x(x):
+    size = lax.axis_size("rows")
+    groups = [[c + (size // 4) * j for j in range(4)] for c in range(size // 4)]
+    copies = jnp.broadcast_to(x[None], (4,) + x.shape)
+    got = lax.all_to_all(copies, "rows", 0, 0, axis_index_groups=groups)
+    return (got[0] + got[1]) + (got[2] + got[3])
+
+
+def core_halves(x):
+    odd = lax.axis_index("rows") % 2 == 1
+    half = x.shape[0] // 2
+    keep = jnp.where(odd, x[half:], x[:half])
+    give = jnp.where(odd, x[:half], x[half:])
+    return keep + swapped(give, 1), odd
+
+
+def both_halves(part, odd):
+    other = swapped(part, 1)
+    return jnp.where(odd, jnp.concatenate([other, part], 0), jnp.concatenate([part, other], 0))
 
 
 def moved(x, distance):
-    devices = range(lax.axis_size("pairs"))
-    return lax.ppermute(x, "pairs", [(i - distance, i) for i in devices if i - distance in devices])
+    count = lax.axis_size("pairs")
+    return lax.ppermute(
+        x, "pairs", [(i - distance, i) for i in range(count) if 0 <= i - distance < count]
+    )
+
+
+def big(a, b, dims):
+    return lax.dot_general(
+        a, b, (dims, ((), ())), precision=lax.Precision.HIGH, preferred_element_type=jnp.float32
+    )
 
 
 def per_device(matrix):
@@ -162,28 +175,47 @@
     first = seat == 0
     last = seat == lax.axis_size("pairs") - 1
     rows_all = matrix.shape[0] * lax.axis_size("rows")
-
-    local = tn(matrix, matrix)
+    early = matrix.shape[0] * EARLY // 16
+
+    local = big(matrix, matrix, ((0,), (0,)))
     packed = jnp.concatenate([local[:BLK, :BLK], local[:BLK, BLK:], local[BLK:, BLK:]], 0)
-    packed = summed_over_rows(packed, True) / rows_all
+    part, odd = core_halves(packed)
+    part = part + swapped(part, 2)
+
+    part, columns = lax.optimization_barrier((part, matrix[:early]))
+    from_left = moved(columns, 1)
+    from_right = moved(columns, -1)
+
+    packed = both_halves(summed_over_x(part), odd) / rows_all
     rotation, gram = eigen_steps(packed[:BLK], packed[BLK : 2 * BLK], packed[2 * BLK :])
 
-    leading = nn(matrix, rotation[:, :BLK])
-    trailing = nn(matrix, rotation[:, BLK:])
+    rotation, gram, from_left, from_right = lax.optimization_barrier(
+        (rotation, gram, from_left, from_right)
+    )
+    to_lead, to_trail = rotation[:, :BLK], rotation[:, BLK:]
     lead_gram, trail_gram = gram[:BLK, :BLK], gram[BLK:, BLK:]
-
-    arrived = moved(jnp.where(first, trailing, leading), 1)
-    from_right = moved(trailing, -1)
-    arrived_gram = moved(jnp.where(first, trail_gram, lead_gram), 1)
-    from_right_gram = moved(trail_gram, -1)
-    new_leading = jnp.where(first, leading, arrived)
-    new_trailing = jnp.where(last, leading, from_right)
-    new_lead_gram = jnp.where(first, lead_gram, arrived_gram)
-    new_trail_gram = jnp.where(last, lead_gram, from_right_gram)
-
-    cross = summed_over_rows(tn(new_leading, new_trailing), False) / rows_all
+    ahead = jnp.where(first, to_trail, to_lead)
+    ahead_gram = jnp.where(first, trail_gram, lead_gram)
+    rest = matrix[early:]
+    over_left = moved(jnp.concatenate([ahead, ahead_gram, big(rest, ahead, ((1,), (0,)))], 0), 1)
+    over_right = moved(
+        jnp.concatenate([to_trail, trail_gram, big(rest, to_trail, ((1,), (0,)))], 0), -1
+    )
+    own = big(matrix, to_lead, ((1,), (0,)))
+    turned_left = big(from_left, over_left[: 2 * BLK], ((1,), (0,)))
+    turned_right = big(from_right, over_right[: 2 * BLK], ((1,), (0,)))
+    new_leading = jnp.where(first, own, jnp.concatenate([turned_left, over_left[3 * BLK :]], 0))
+    new_trailing = jnp.where(last, own, jnp.concatenate([turned_right, over_right[3 * BLK :]], 0))
+    new_lead_gram = jnp.where(first, lead_gram, over_left[2 * BLK : 3 * BLK])
+    new_trail_gram = jnp.where(last, lead_gram, over_right[2 * BLK : 3 * BLK])
+
+    cross = big(new_leading, new_trailing, ((0,), (0,)))
+    cross = cross + swapped(cross, 1)
+    cross = summed_over_x(cross)
+    cross = (cross + swapped(cross, 2)) / rows_all
     rotation, gram = eigen_steps(new_lead_gram, cross, new_trail_gram)
-    paired = nn(new_leading, rotation[:BLK]) + nn(new_trailing, rotation[BLK:])
+    paired = big(new_leading, rotation[:BLK], ((1,), (0,)))
+    paired = paired + big(new_trailing, rotation[BLK:], ((1,), (0,)))
     return paired, gram
 
 

time: 193 us -> 168 us (0.87)
  the two profiles are of different devices: /device:TPU:248 before, /device:TPU:504 now
where the time goes in v2:
time: 168 us; the launch traced here: 167 us
  waiting for transfers between devices  59.3 us (35%)
  Pallas kernels  49.3 us (29%)
  starting transfers between devices  26.6 us (16%)
  matrix products  14 us (8%)
  blocking collectives  11.6 us (7%)
  other arithmetic  3.05 us (2%)
  local copies, waits for them, and re-layouts  2.08 us (1%)
    pallas_call x2, Pallas kernels, eigen_steps(): pl.pallas_call(eigen_kernel, out_shape=(full, full), in_specs=[vmem] * 3,...  49.3 us
    ppermute x4, waiting for transfers between devices, moved(): lax.ppermute(x, 'pairs', [(i - distance, i) for i in range(count) if 0 <=...  38.3 us
    ppermute x5, waiting for transfers between devices, swapped(): lax.ppermute(x, 'rows', [(i, i ^ bit) for i in range(lax.axis_size('rows'...  18.3 us
    dot_general x9, matrix products, big(): lax.dot_general(a, b, (dims, ((), ())), precision=lax.Precision.HIGH, pre...  14 us
    ppermute x5, starting transfers between devices, swapped(): lax.ppermute(x, 'rows', [(i, i ^ bit) for i in range(lax.axis_size('rows'...  13.1 us
    all_to_all x1, blocking collectives, summed_over_x(): got = lax.all_to_all(copies, 'rows', 0, 0, axis_index_groups=groups)  11.6 us
    ppermute x4, starting transfers between devices, moved(): lax.ppermute(x, 'pairs', [(i - distance, i) for i in range(count) if 0 <=...  9.14 us
    all_to_all x1, starting transfers between devices, summed_over_x(): got = lax.all_to_all(copies, 'rows', 0, 0, axis_index_groups=groups)  4.29 us
  transfers between devices with their start and end apart: 10, of which 8 were waited for; matrix products, arithmetic and copies ran while one was open for 3% of the time, Pallas kernels for 15%

profile of v2, /device:TPU:504, one launch (start us, length us, event | category | flops | bytes accessed | tf_op | source)
XLA Modules:
  0.0 166.8 jit_solution(15574236998556452458)
XLA Ops:
  0.6 4.2 %fusion.21 = f32[256,256]{1,0:T(8,128)S(1)} fusion(f32[2048,256]{1,0:T(8,128)} %param.1), kind=kOutput, calls=%fused_computation.42 | convolution fusion | flops 805306368 | bytes 2359296 | tf_op jit(solution)/shard_map/dot_general | solution.py:168
  4.9 1.9 %collective-permute-start = (f32[192,128]{1,0:T(8,128)S(1)}, f32[192,128]{1,0:T(8,128)S(1)}, u32[]{:S(2)}, u32[]{:S(2)}) collective-permute-start(f32[192,128]{1,0:T(8,128)S(1)} %slice_select_fusion.1), channel_id=1, source_target_pairs={{0,1},{1,0},{2,3},{3,2},{4,5},{5,4},{6,7},{7,6},{8,9},{9,8},{10,11... | collective-permute-start | bytes 294920 | tf_op jit(solution)/shard_map/ppermute | solution.py:136
  6.8 1.3 collective-permute-done
  8.1 4.7 %collective-permute-start.1 = (f32[192,128]{1,0:T(8,128)S(1)}, f32[192,128]{1,0:T(8,128)S(1)}, u32[]{:S(2)}, u32[]{:S(2)}) collective-permute-start(f32[192,128]{1,0:T(8,128)S(1)} %select_add_fusion), channel_id=1, source_target_pairs={{0,2},{1,3},{2,0},{3,1},{4,6},{5,7},{6,4},{7,5},{8,10},{9,11},{10,... | collective-permute-start | bytes 294920 | tf_op jit(solution)/shard_map/ppermute | solution.py:136
  12.9 8.0 %collective-permute-done.1 = f32[192,128]{1,0:T(8,128)S(1)} collective-permute-done((f32[192,128]{1,0:T(8,128)S(1)}, f32[192,128]{1,0:T(8,128)S(1)}, u32[]{:S(2)}, u32[]{:S(2)}) %collective-permute-start.1) | collective-permute-done | bytes 98336 | tf_op jit(solution)/shard_map/ppermute | solution.py:136
  21.7 4.3 %all-to-all-start = ((f32[4,192,128]{2,1,0:T(8,128)}), f32[4,192,128]{2,1,0:T(8,128)S(1)}, u32[]{:S(2)}, u32[]{:S(2)}) async-start(f32[4,192,128]{2,1,0:T(8,128)} %broadcast_in_dim.4), calls=%async_computation | async-start | bytes 786432 | tf_op jit(solution)/shard_map/all_to_all | solution.py:143
  26.0 3.9 %collective-permute-start.4 = (f32[640,256]{1,0:T(8,128)S(1)}, f32[640,256]{1,0:T(8,128)}, u32[]{:S(2)}, u32[]{:S(2)}) collective-permute-start(f32[640,256]{1,0:T(8,128)S(1)} %slice.97), channel_id=1, source_target_pairs={{16,0},{32,16},{48,32},{64,48},{80,64},{96,80},{112,96},{128,112},... | collective-permute-start | bytes 1966088 | tf_op jit(solution)/shard_map/ppermute | solution.py:162
  29.9 1.3 collective-permute-start.3
  31.2 2.8 %all-to-all-done = f32[4,192,128]{2,1,0:T(8,128)S(1)} async-done(((f32[4,192,128]{2,1,0:T(8,128)}), f32[4,192,128]{2,1,0:T(8,128)S(1)}, u32[]{:S(2)}, u32[]{:S(2)}) %all-to-all-start) | async-done | bytes 393248 | tf_op jit(solution)/shard_map/all_to_all | solution.py:143
  34.0 1.9 %collective-permute-start.2 = (f32[192,128]{1,0:T(8,128)S(1)}, f32[192,128]{1,0:T(8,128)S(1)}, u32[]{:S(2)}, u32[]{:S(2)}) collective-permute-start(f32[192,128]{1,0:T(8,128)S(1)} %fusion.13), channel_id=1, source_target_pairs={{0,1},{1,0},{2,3},{3,2},{4,5},{5,4},{6,7},{7,6},{8,9},{9,8},{10,11... | collective-permute-start | bytes 294920 | tf_op jit(solution)/shard_map/ppermute | solution.py:136
  35.9 1.3 collective-permute-done.2
  37.3 24.3 %eigen_steps.2 = (f32[256,256]{1,0:T(8,128)S(1)}, f32[256,256]{1,0:T(8,128)S(1)}) custom-call(f32[128,128]{1,0:T(8,128)S(1)} %get-tuple-element.30.lead_ref, f32[128,128]{1,0:T(8,128)S(1)} %get-tuple-element.29.cross_ref, f32[128,128]{1,0:T(8,128)S(1)} %get-tuple-element.28.trail_ref), custom_call_target="tpu_custom_call" | custom-call | tf_op jit(solution)/shard_map/eigen_steps/pallas_call | solution.py:124
  63.3 2.5 %collective-permute-start.6 = (f32[1792,128]{1,0:T(8,128)}, f32[1792,128]{1,0:T(8,128)S(1)}, u32[]{:S(2)}, u32[]{:S(2)}) collective-permute-start(f32[1792,128]{1,0:T(8,128)} %pad_maximum_fusion.1), channel_id=1, source_target_pairs={{16,0},{32,16},{48,32},{64,48},{80,64},{96,80},{112,96},{128,112},... | collective-permute-start | bytes 2752520 | tf_op jit(solution)/shard_map/ppermute | solution.py:162
  67.6 1.5 collective-permute-start.5
  70.1 15.9 %collective-permute-done.6 = f32[1792,128]{1,0:T(8,128)S(1)} collective-permute-done((f32[1792,128]{1,0:T(8,128)}, f32[1792,128]{1,0:T(8,128)S(1)}, u32[]{:S(2)}, u32[]{:S(2)}) %collective-permute-start.6) | collective-permute-done | bytes 917536 | tf_op jit(solution)/shard_map/ppermute | solution.py:162
  86.0 1.5 fusion.5
  87.5 22.4 %collective-permute-done.5 = f32[1792,128]{1,0:T(8,128)} collective-permute-done((f32[1792,128]{1,0:T(8,128)}, f32[1792,128]{1,0:T(8,128)}, u32[]{:S(2)}, u32[]{:S(2)}) %collective-permute-start.5) | collective-permute-done | bytes 917536 | tf_op jit(solution)/shard_map/ppermute | solution.py:162
  111.1 1.5 fusion.7
  113.6 1.9 %collective-permute-start.7 = (f32[128,128]{1,0:T(8,128)S(1)}, f32[128,128]{1,0:T(8,128)S(1)}, u32[]{:S(2)}, u32[]{:S(2)}) collective-permute-start(f32[128,128]{1,0:T(8,128)S(1)} %fusion.3), channel_id=1, source_target_pairs={{0,1},{1,0},{2,3},{3,2},{4,5},{5,4},{6,7},{7,6},{8,9},{9,8},{10,11... | collective-permute-start | bytes 196616 | tf_op jit(solution)/shard_map/ppermute | solution.py:136
  116.8 11.6 %all_to_all.10 = f32[4,128,128]{2,1,0:T(8,128)S(1)} all-to-all(f32[4,128,128]{2,1,0:T(8,128)S(1)} %broadcast_in_dim.5), channel_id=1, replica_groups={{0,4,8,12},{1,5,9,13},{2,6,10,14},{3,7,11,15},{16,20,24,28},{17,21,25,2..., dimensions={0} | all-to-all | bytes 524288 | tf_op jit(solution)/shard_map/all_to_all | solution.py:143
  128.4 2.7 %collective-permute-start.8 = (f32[128,128]{1,0:T(8,128)S(1)}, f32[128,128]{1,0:T(8,128)S(1)}, u32[]{:S(2)}, u32[]{:S(2)}) collective-permute-start(f32[128,128]{1,0:T(8,128)S(1)} %fusion.15), channel_id=1, source_target_pairs={{0,2},{1,3},{2,0},{3,1},{4,6},{5,7},{6,4},{7,5},{8,10},{9,11},{10,... | collective-permute-start | bytes 196616 | tf_op jit(solution)/shard_map/ppermute | solution.py:136
  132.0 6.5 %collective-permute-done.8 = f32[128,128]{1,0:T(8,128)S(1)} collective-permute-done((f32[128,128]{1,0:T(8,128)S(1)}, f32[128,128]{1,0:T(8,128)S(1)}, u32[]{:S(2)}, u32[]{:S(2)}) %collective-permute-start.8) | collective-permute-done | bytes 65568 | tf_op jit(solution)/shard_map/ppermute | solution.py:136
  138.5 25.0 %eigen_steps.3 = (f32[256,256]{1,0:T(8,128)S(1)}, f32[256,256]{1,0:T(8,128)}) custom-call(f32[128,128]{1,0:T(8,128)S(1)} %get-tuple-element.23.lead_ref, f32[128,128]{1,0:T(8,128)S(1)} %add_multiply_fusion.cross_ref, f32[128,128]{1,0:T(8,128)S(1)} %get-tuple-element.22.trail_ref), custom_call_target="tpu_custom_call" | custom-call | tf_op jit(solution)/shard_map/eigen_steps/pallas_call | solution.py:124
  164.5 2.3 %convolution_add_fusion = f32[2048,256]{1,0:T(8,128)} fusion(f32[2048,256]{1,0:T(8,128)S(1)} %fusion.2, f32[2048,128]{1,0:T(8,128)S(1)} %convolution_bitcast_fusion.2, f32[1408,128]{1,0:T(8,128)S(1)} %slice.133, f32[640,128]{1,0:T(8,128)S(1)} %fusion.7, pred[]{:T(512)S(6)} %eq.11, f32[256,256]{1,0:T(8,128)S(1)} %get-tuple-element.20), kind=kOutput, calls=%fused_computation | convolution fusion | flops 403701760 | bytes 6422529 | tf_op jit(solution)/shard_map/dot_general | solution.py:168
  (31 shorter events, 10.8 us)
Async XLA Ops:
  0.6 12.2 %copy-start = (f32[2048,256]{1,0:T(8,128)S(1)}, f32[2048,256]{1,0:T(8,128)}, u32[]{:S(2)}) copy-start(f32[2048,256]{1,0:T(8,128)} %param.1) | copy-start | bytes 6291460
  4.9 3.2 %collective-permute-start = (f32[192,128]{1,0:T(8,128)S(1)}, f32[192,128]{1,0:T(8,128)S(1)}, u32[]{:S(2)}, u32[]{:S(2)}) collective-permute-start(f32[192,128]{1,0:T(8,128)S(1)} %slice_select_fusion.1), channel_id=1, source_target_pairs={{0,1},{1,0},{2,3},{3,2},{4,5},{5,4},{6,7},{7,6},{8,9},{9,8},{10,11... | collective-permute-start | bytes 294920 | tf_op jit(solution)/shard_map/ppermute | solution.py:136
  8.1 12.8 %collective-permute-start.1 = (f32[192,128]{1,0:T(8,128)S(1)}, f32[192,128]{1,0:T(8,128)S(1)}, u32[]{:S(2)}, u32[]{:S(2)}) collective-permute-start(f32[192,128]{1,0:T(8,128)S(1)} %select_add_fusion), channel_id=1, source_target_pairs={{0,2},{1,3},{2,0},{3,1},{4,6},{5,7},{6,4},{7,5},{8,10},{9,11},{10,... | collective-permute-start | bytes 294920 | tf_op jit(solution)/shard_map/ppermute | solution.py:136
  21.7 12.3 %all-to-all-start = ((f32[4,192,128]{2,1,0:T(8,128)}), f32[4,192,128]{2,1,0:T(8,128)S(1)}, u32[]{:S(2)}, u32[]{:S(2)}) async-start(f32[4,192,128]{2,1,0:T(8,128)} %broadcast_in_dim.4), calls=%async_computation | async-start | bytes 786432 | tf_op jit(solution)/shard_map/all_to_all | solution.py:143
  26.0 35.6 %collective-permute-start.4 = (f32[640,256]{1,0:T(8,128)S(1)}, f32[640,256]{1,0:T(8,128)}, u32[]{:S(2)}, u32[]{:S(2)}) collective-permute-start(f32[640,256]{1,0:T(8,128)S(1)} %slice.97), channel_id=1, source_target_pairs={{16,0},{32,16},{48,32},{64,48},{80,64},{96,80},{112,96},{128,112},... | collective-permute-start | bytes 1966088 | tf_op jit(solution)/shard_map/ppermute | solution.py:162
  29.9 31.7 %collective-permute-start.3 = (f32[640,256]{1,0:T(8,128)S(1)}, f32[640,256]{1,0:T(8,128)}, u32[]{:S(2)}, u32[]{:S(2)}) collective-permute-start(f32[640,256]{1,0:T(8,128)S(1)} %slice.97), channel_id=1, source_target_pairs={{0,16},{16,32},{32,48},{48,64},{64,80},{80,96},{96,112},{112,128},... | collective-permute-start | bytes 1966088 | tf_op jit(solution)/shard_map/ppermute | solution.py:162
  34.0 3.2 %collective-permute-start.2 = (f32[192,128]{1,0:T(8,128)S(1)}, f32[192,128]{1,0:T(8,128)S(1)}, u32[]{:S(2)}, u32[]{:S(2)}) collective-permute-start(f32[192,128]{1,0:T(8,128)S(1)} %fusion.13), channel_id=1, source_target_pairs={{0,1},{1,0},{2,3},{3,2},{4,5},{5,4},{6,7},{7,6},{8,9},{9,8},{10,11... | collective-permute-start | bytes 294920 | tf_op jit(solution)/shard_map/ppermute | solution.py:136
  63.3 22.6 %collective-permute-start.6 = (f32[1792,128]{1,0:T(8,128)}, f32[1792,128]{1,0:T(8,128)S(1)}, u32[]{:S(2)}, u32[]{:S(2)}) collective-permute-start(f32[1792,128]{1,0:T(8,128)} %pad_maximum_fusion.1), channel_id=1, source_target_pairs={{16,0},{32,16},{48,32},{64,48},{80,64},{96,80},{112,96},{128,112},... | collective-permute-start | bytes 2752520 | tf_op jit(solution)/shard_map/ppermute | solution.py:162
  67.6 42.3 %collective-permute-start.5 = (f32[1792,128]{1,0:T(8,128)}, f32[1792,128]{1,0:T(8,128)}, u32[]{:S(2)}, u32[]{:S(2)}) collective-permute-start(f32[1792,128]{1,0:T(8,128)} %pad_maximum_fusion), channel_id=1, source_target_pairs={{0,16},{16,32},{32,48},{48,64},{64,80},{80,96},{96,112},{112,128},... | collective-permute-start | bytes 2752520 | tf_op jit(solution)/shard_map/ppermute | solution.py:162
  113.6 3.1 %collective-permute-start.7 = (f32[128,128]{1,0:T(8,128)S(1)}, f32[128,128]{1,0:T(8,128)S(1)}, u32[]{:S(2)}, u32[]{:S(2)}) collective-permute-start(f32[128,128]{1,0:T(8,128)S(1)} %fusion.3), channel_id=1, source_target_pairs={{0,1},{1,0},{2,3},{3,2},{4,5},{5,4},{6,7},{7,6},{8,9},{9,8},{10,11... | collective-permute-start | bytes 196616 | tf_op jit(solution)/shard_map/ppermute | solution.py:136
  128.4 10.1 %collective-permute-start.8 = (f32[128,128]{1,0:T(8,128)S(1)}, f32[128,128]{1,0:T(8,128)S(1)}, u32[]{:S(2)}, u32[]{:S(2)}) collective-permute-start(f32[128,128]{1,0:T(8,128)S(1)} %fusion.15), channel_id=1, source_target_pairs={{0,2},{1,3},{2,0},{3,1},{4,6},{5,7},{6,4},{7,5},{8,10},{9,11},{10,... | collective-permute-start | bytes 196616 | tf_op jit(solution)/shard_map/ppermute | solution.py:136

commit v3 on v2

--- a/solution.py
+++ b/solution.py
@@ -8,8 +8,12 @@
 ITERS = 3
 BLK = 128
 SUB = 8
-TILES = BLK // SUB
+LANES = 128
+PANEL = 64
 WIDE = 2
+SQUARE = 2
+TURN = 3
+AHEAD = 2
 EARLY = 5
 
 highest = lax.Precision.HIGHEST
@@ -34,87 +38,158 @@
 
 
 def lane(x, k):
-    return jnp.broadcast_to(x[:, k : k + 1], (SUB, BLK))
+    return jnp.broadcast_to(x[:, k : k + 1], (SUB, LANES))
 
 
 def row(x, k):
-    return jnp.broadcast_to(x[k : k + 1, :], (SUB, BLK))
-
-
-def inverse_factor(square):
-    lanes = lax.broadcasted_iota(jnp.int32, (SUB, BLK), 1)
-    rows = lax.broadcasted_iota(jnp.int32, (SUB, BLK), 0)
-    s = [square[SUB * q : SUB * q + SUB, :] for q in range(TILES)]
-    w = [None] * TILES
-    for p in range(0, TILES, WIDE):
-        count = SUB * WIDE
+    return jnp.broadcast_to(x[k : k + 1, :], (SUB, LANES))
+
+
+def inverse_factors(squares, wide, beside):
+    lanes = lax.broadcasted_iota(jnp.int32, (SUB, LANES), 1)
+    rows = lax.broadcasted_iota(jnp.int32, (SUB, LANES), 0)
+    blank = jnp.zeros((SUB, LANES - PANEL), jnp.float32)
+    tiles = PANEL // SUB
+    tables = [
+        [jnp.concatenate([s[SUB * q : SUB * q + SUB, :], blank], 1) for q in range(tiles)]
+        for s in squares
+    ]
+    factors = [[None] * tiles for _ in squares]
+    count = SUB * wide
+    for p in range(0, tiles, wide):
         low = SUB * p
         inside = (lanes >= low) & (lanes < low + count)
-        c = [[lane(s[p + r], low + k) for r in range(WIDE)] for k in range(count)]
-        a = [
-            jnp.where(inside, jnp.where(lanes == rows + SUB * (p + r), 1.0, 0.0), s[p + r])
-            for r in range(WIDE)
-        ]
-        done = [None] * WIDE
-        scale = [None] * WIDE
+        states = []
+        for s in tables:
+            c = [[lane(s[p + r], low + k) for r in range(wide)] for k in range(count)]
+            a = [
+                jnp.where(inside, jnp.where(lanes == rows + SUB * (p + r), 1.0, 0.0), s[p + r])
+                for r in range(wide)
+            ]
+            states.append((c, a, [None] * wide, [None] * wide))
         for k in range(count):
+            next(beside, None)
             t, j = divmod(k, SUB)
-            pivot = row(c[k][t], j)
-            inv = 1.0 / pivot
-            z = row(a[t], j)
-            finished = z * lax.rsqrt(pivot)
-            done[t] = finished if j == 0 else jnp.where(rows == j, finished, done[t])
-            scale[t] = inv if j == 0 else jnp.where(rows == j, inv, scale[t])
-            column = list(c[k])
-            column[t] = jnp.where(rows == j, 0.0, column[t])
-            factor = [column[r] * inv for r in range(WIDE)]
-            for l in range(k + 1, count):
-                m = row(c[l][t], j)
-                for r in range(WIDE):
-                    c[l][r] = c[l][r] - factor[r] * m
-            for r in range(WIDE):
-                a[r] = a[r] - factor[r] * z
-        for r in range(WIDE):
-            w[p + r] = jnp.where(lanes <= rows + SUB * (p + r), done[r], 0.0)
-        if p + WIDE < TILES:
-            y = [a[r] * scale[r] for r in range(WIDE)]
-            ys = [row(y[k // SUB], k % SUB) for k in range(count)]
-            for q in range(p + WIDE, TILES):
-                o = [lane(s[q], low + k) for k in range(count)]
-                even = o[0] * ys[0]
-                odd = o[1] * ys[1]
-                for k in range(2, count, 2):
-                    even = even + o[k] * ys[k]
-                    odd = odd + o[k + 1] * ys[k + 1]
-                s[q] = jnp.where(inside, 0.0, s[q]) - (even + odd)
-    return jnp.concatenate(w, 0)
-
-
-def eigen_kernel(lead_ref, cross_ref, trail_ref, rotation_ref, gram_ref, g, z):
+            for c, a, done, scale in states:
+                pivot = row(c[k][t], j)
+                inv = 1.0 / pivot
+                z = row(a[t], j)
+                finished = z * lax.rsqrt(pivot)
+                done[t] = finished if j == 0 else jnp.where(rows == j, finished, done[t])
+                scale[t] = inv if j == 0 else jnp.where(rows == j, inv, scale[t])
+                column = list(c[k])
+                column[t] = jnp.where(rows == j, 0.0, column[t])
+                factor = [column[r] * inv for r in range(wide)]
+                for l in range(k + 1, count):
+                    m = row(c[l][t], j)
+                    for r in range(wide):
+                        c[l][r] = c[l][r] - factor[r] * m
+                for r in range(wide):
+                    a[r] = a[r] - factor[r] * z
+        for s, w, (c, a, done, scale) in zip(tables, factors, states):
+            for r in range(wide):
+                w[p + r] = jnp.where(lanes <= rows + SUB * (p + r), done[r], 0.0)
+            if p + wide < tiles:
+                y = [a[r] * scale[r] for r in range(wide)]
+                ys = [row(y[k // SUB], k % SUB) for k in range(count)]
+                for q in range(p + wide, tiles):
+                    o = [lane(s[q], low + k) for k in range(count)]
+                    even = o[0] * ys[0]
+                    odd = o[1] * ys[1]
+                    for k in range(2, count, 2):
+                        even = even + o[k] * ys[k]
+                        odd = odd + o[k + 1] * ys[k + 1]
+                    s[q] = jnp.where(inside, 0.0, s[q]) - (even + odd)
+    for _ in beside:
+        pass
+    return [jnp.concatenate(w, 0)[:, :PANEL] for w in factors]
+
+
+def parts(x, count):
+    found = []
+    for _ in range(count - 1):
+        head = x.astype(jnp.bfloat16)
+        found.append(head)
+        x = x - head.astype(jnp.float32)
+    return found + [x.astype(jnp.bfloat16)]
+
+
+def product_steps(a, b, dims):
+    count = min(len(a), len(b))
+    total = None
+    for order in reversed(range(count)):
+        for i in range(order + 1):
+            term = lax.dot_general(
+                a[i], b[order - i], (dims, ((), ())), preferred_element_type=jnp.float32
+            )
+            total = term if total is None else total + term
+            yield
+    return total
+
+
+def product(a, b, dims):
+    steps = product_steps(a, b, dims)
+    while True:
+        try:
+            next(steps)
+        except StopIteration as end:
+            return end.value
+
+
+def ahead_steps(states, known, fixed, found):
+    for t, x, along in states:
+        if along is not None:
+            x = x - (yield from product_steps(along, known[t], NN))
+        far = yield from product_steps(parts(x, AHEAD), fixed, NN)
+        found.append(parts(jnp.concatenate([x, far], 1), TURN))
+
+
+NN = ((1,), (0,))
+NT = ((1,), (1,))
+
+
+def eigen_kernel(lead_ref, cross_ref, trail_ref, rotation_ref, gram_ref, g, turns, z):
+    cross = cross_ref[...]
     g[:BLK, :BLK] = lead_ref[...]
-    g[:BLK, BLK:] = cross_ref[...]
-    g[BLK:, :BLK] = cross_ref[...].T
+    g[:BLK, BLK:] = cross
+    g[BLK:, :BLK] = cross.T
     g[BLK:, BLK:] = trail_ref[...]
-    z[...] = g[...]
-
-    def sweep(_, carry):
-        za, zc = z[:, :BLK], z[:, BLK:]
-        saa = tn(za, za)
-        sac = tn(za, zc)
-        scc = tn(zc, zc)
-        wa = inverse_factor(saa)
-        t = nn(wa, sac)
-        va = nt(za, wa)
-        xc = zc - nn(va, t)
-        wc = inverse_factor(scc - tn(t, t))
-        vc = nt(xc, wc)
-        rotation_ref[:, :BLK] = va
-        rotation_ref[:, BLK:] = vc
-        z[...] = nn(g[...], rotation_ref[...])
-        return carry
-
-    lax.fori_loop(0, ITERS, sweep, 0)
-    final = tn(rotation_ref[...], z[...])
+    panels = 2 * BLK // PANEL
+    fixed = parts(g[...], AHEAD)
+    ready = {(0, j): g[PANEL * j : PANEL * j + PANEL, :] for j in range(panels)}
+    known = {t: None for t in range(ITERS)}
+    for stage in range(panels + ITERS - 1):
+        active = [(t, stage - t) for t in range(ITERS) if 0 <= stage - t < panels]
+        squares, states = [], []
+        for t, j in active:
+            x = ready.pop((t, j))
+            split = parts(x, SQUARE)
+            square = product(split, split, NT)
+            along = None
+            if j > 0:
+                along = parts(product(split, known[t], NT), SQUARE)
+                square = square - product(along, along, NT)
+            squares.append(square)
+            states.append((t, x, along))
+        found = []
+        factors = inverse_factors(squares, WIDE, ahead_steps(states, known, fixed, found))
+        for (t, j), both, w in zip(active, found, factors):
+            both = product(parts(w, TURN), both, NN)
+            turn, ahead = both[:, : 2 * BLK], both[:, 2 * BLK :]
+            turns[t, PANEL * j : PANEL * j + PANEL, :] = turn
+            if j + 1 < panels:
+                split = parts(turn, SQUARE)
+                old = known[t]
+                known[t] = split if old is None else [
+                    jnp.concatenate([a, b], 0) for a, b in zip(old, split)
+                ]
+            if t + 1 < ITERS:
+                ready[t + 1, j] = ahead
+            else:
+                z[PANEL * j : PANEL * j + PANEL, :] = ahead
+    turned = turns[ITERS - 1]
+    final = product(parts(turned, AHEAD), parts(z[...], AHEAD), NT)
+    rotation_ref[...] = turned.T
     gram_ref[...] = 0.5 * (final + final.T)
 
 
@@ -126,7 +201,11 @@
         out_shape=(full, full),
         in_specs=[vmem] * 3,
         out_specs=(vmem, vmem),
-        scratch_shapes=[pltpu.VMEM((2 * BLK, 2 * BLK), jnp.float32)] * 2,
+        scratch_shapes=[
+            pltpu.VMEM((2 * BLK, 2 * BLK), jnp.float32),
+            pltpu.VMEM((ITERS, 2 * BLK, 2 * BLK), jnp.float32),
+            pltpu.VMEM((2 * BLK, 2 * BLK), jnp.float32),
+        ],
         compiler_params=pltpu.CompilerParams(vmem_limit_bytes=32 * 1024 * 1024),
         name="eigen_steps",
     )(lead, cross, trail)

time: 168 us -> 157 us (0.935)
  Pallas kernels: 49.3 us -> 33.3 us
  waiting for transfers between devices: 59.3 us -> 65.5 us
    pallas_call x2, Pallas kernels: 49.3 us -> 33.3 us  [eigen_steps(): pl.pallas_call(eigen_kernel, out_shape=(full, full), in_specs=[vmem] * 3,...]
    ppermute x4, waiting for transfers between devices: 38.3 us -> 44.1 us  [moved(): lax.ppermute(x, 'pairs', [(i - distance, i) for i in range(count) if 0 <=...]
  transfers between devices with their start and end apart: 10 -> 10, of which waited for: 8 -> 9; matrix products, arithmetic and copies ran while one was open for 3% -> 3% of each run, Pallas kernels for 15% -> 10%
where the time goes in v3:
time: 157 us; the launch traced here: 156 us
  waiting for transfers between devices  65.5 us (42%)
  Pallas kernels  33.3 us (21%)
  starting transfers between devices  26.1 us (17%)
  matrix products  14 us (9%)
  blocking collectives  11.3 us (7%)
  other arithmetic  3.05 us (2%)
  local copies, waits for them, and re-layouts  2.08 us (1%)
    ppermute x4, waiting for transfers between devices, moved(): lax.ppermute(x, 'pairs', [(i - distance, i) for i in range(count) if 0 <=...  44.1 us
    pallas_call x2, Pallas kernels, eigen_steps(): pl.pallas_call(eigen_kernel, out_shape=(full, full), in_specs=[vmem] * 3,...  33.3 us
    ppermute x5, waiting for transfers between devices, swapped(): lax.ppermute(x, 'rows', [(i, i ^ bit) for i in range(lax.axis_size('rows'...  18.6 us
    dot_general x9, matrix products, big(): lax.dot_general(a, b, (dims, ((), ())), precision=lax.Precision.HIGH, pre...  14 us
    ppermute x5, starting transfers between devices, swapped(): lax.ppermute(x, 'rows', [(i, i ^ bit) for i in range(lax.axis_size('rows'...  12.8 us
    all_to_all x1, blocking collectives, summed_over_x(): got = lax.all_to_all(copies, 'rows', 0, 0, axis_index_groups=groups)  11.3 us
    ppermute x4, starting transfers between devices, moved(): lax.ppermute(x, 'pairs', [(i - distance, i) for i in range(count) if 0 <=...  8.99 us
    all_to_all x1, starting transfers between devices, summed_over_x(): got = lax.all_to_all(copies, 'rows', 0, 0, axis_index_groups=groups)  4.29 us
  transfers between devices with their start and end apart: 10, of which 9 were waited for; matrix products, arithmetic and copies ran while one was open for 3% of the time, Pallas kernels for 10%

profile of v3, /device:TPU:504, one launch (start us, length us, event | category | flops | bytes accessed | tf_op | source)
XLA Modules:
  0.0 156.2 jit_solution(6888433512329963894)
XLA Ops:
  0.6 4.2 %fusion.21 = f32[256,256]{1,0:T(8,128)S(1)} fusion(f32[2048,256]{1,0:T(8,128)} %param.1), kind=kOutput, calls=%fused_computation.42 | convolution fusion | flops 805306368 | bytes 2359296 | tf_op jit(solution)/shard_map/dot_general | solution.py:247
  4.9 1.9 %collective-permute-start = (f32[192,128]{1,0:T(8,128)S(1)}, f32[192,128]{1,0:T(8,128)S(1)}, u32[]{:S(2)}, u32[]{:S(2)}) collective-permute-start(f32[192,128]{1,0:T(8,128)S(1)} %slice_select_fusion.1), channel_id=1, source_target_pairs={{0,1},{1,0},{2,3},{3,2},{4,5},{5,4},{6,7},{7,6},{8,9},{9,8},{10,11... | collective-permute-start | bytes 294920 | tf_op jit(solution)/shard_map/ppermute | solution.py:215
  6.8 1.3 collective-permute-done
  8.1 4.7 %collective-permute-start.1 = (f32[192,128]{1,0:T(8,128)S(1)}, f32[192,128]{1,0:T(8,128)S(1)}, u32[]{:S(2)}, u32[]{:S(2)}) collective-permute-start(f32[192,128]{1,0:T(8,128)S(1)} %select_add_fusion), channel_id=1, source_target_pairs={{0,2},{1,3},{2,0},{3,1},{4,6},{5,7},{6,4},{7,5},{8,10},{9,11},{10,... | collective-permute-start | bytes 294920 | tf_op jit(solution)/shard_map/ppermute | solution.py:215
  12.9 8.0 %collective-permute-done.1 = f32[192,128]{1,0:T(8,128)S(1)} collective-permute-done((f32[192,128]{1,0:T(8,128)S(1)}, f32[192,128]{1,0:T(8,128)S(1)}, u32[]{:S(2)}, u32[]{:S(2)}) %collective-permute-start.1) | collective-permute-done | bytes 98336 | tf_op jit(solution)/shard_map/ppermute | solution.py:215
  21.7 4.3 %all-to-all-start = ((f32[4,192,128]{2,1,0:T(8,128)}), f32[4,192,128]{2,1,0:T(8,128)S(1)}, u32[]{:S(2)}, u32[]{:S(2)}) async-start(f32[4,192,128]{2,1,0:T(8,128)} %broadcast_in_dim.4), calls=%async_computation | async-start | bytes 786432 | tf_op jit(solution)/shard_map/all_to_all | solution.py:222
  26.0 3.9 %collective-permute-start.4 = (f32[640,256]{1,0:T(8,128)S(1)}, f32[640,256]{1,0:T(8,128)}, u32[]{:S(2)}, u32[]{:S(2)}) collective-permute-start(f32[640,256]{1,0:T(8,128)S(1)} %slice.97), channel_id=1, source_target_pairs={{16,0},{32,16},{48,32},{64,48},{80,64},{96,80},{112,96},{128,112},... | collective-permute-start | bytes 1966088 | tf_op jit(solution)/shard_map/ppermute | solution.py:241
  29.9 1.3 collective-permute-start.3
  31.2 2.8 %all-to-all-done = f32[4,192,128]{2,1,0:T(8,128)S(1)} async-done(((f32[4,192,128]{2,1,0:T(8,128)}), f32[4,192,128]{2,1,0:T(8,128)S(1)}, u32[]{:S(2)}, u32[]{:S(2)}) %all-to-all-start) | async-done | bytes 393248 | tf_op jit(solution)/shard_map/all_to_all | solution.py:222
  34.0 2.1 %collective-permute-start.2 = (f32[192,128]{1,0:T(8,128)S(1)}, f32[192,128]{1,0:T(8,128)S(1)}, u32[]{:S(2)}, u32[]{:S(2)}) collective-permute-start(f32[192,128]{1,0:T(8,128)S(1)} %fusion.13), channel_id=1, source_target_pairs={{0,1},{1,0},{2,3},{3,2},{4,5},{5,4},{6,7},{7,6},{8,9},{9,8},{10,11... | collective-permute-start | bytes 294920 | tf_op jit(solution)/shard_map/ppermute | solution.py:215
  37.3 16.3 %eigen_steps.2 = (f32[256,256]{1,0:T(8,128)S(1)}, f32[256,256]{1,0:T(8,128)S(1)}) custom-call(f32[128,128]{1,0:T(8,128)S(1)} %get-tuple-element.30.lead_ref, f32[128,128]{1,0:T(8,128)S(1)} %get-tuple-element.29.cross_ref, f32[128,128]{1,0:T(8,128)S(1)} %get-tuple-element.28.trail_ref), custom_call_target="tpu_custom_call" | custom-call | tf_op jit(solution)/shard_map/eigen_steps/pallas_call | solution.py:199
  53.5 6.4 %collective-permute-done.3 = f32[640,256]{1,0:T(8,128)} collective-permute-done((f32[640,256]{1,0:T(8,128)S(1)}, f32[640,256]{1,0:T(8,128)}, u32[]{:S(2)}, u32[]{:S(2)}) %collective-permute-start.3) | collective-permute-done | bytes 655392 | tf_op jit(solution)/shard_map/ppermute | solution.py:241
  61.7 2.5 %collective-permute-start.6 = (f32[1792,128]{1,0:T(8,128)}, f32[1792,128]{1,0:T(8,128)S(1)}, u32[]{:S(2)}, u32[]{:S(2)}) collective-permute-start(f32[1792,128]{1,0:T(8,128)} %pad_maximum_fusion.1), channel_id=1, source_target_pairs={{16,0},{32,16},{48,32},{64,48},{80,64},{96,80},{112,96},{128,112},... | collective-permute-start | bytes 2752520 | tf_op jit(solution)/shard_map/ppermute | solution.py:241
  66.0 1.3 collective-permute-start.5
  68.3 15.9 %collective-permute-done.6 = f32[1792,128]{1,0:T(8,128)S(1)} collective-permute-done((f32[1792,128]{1,0:T(8,128)}, f32[1792,128]{1,0:T(8,128)S(1)}, u32[]{:S(2)}, u32[]{:S(2)}) %collective-permute-start.6) | collective-permute-done | bytes 917536 | tf_op jit(solution)/shard_map/ppermute | solution.py:241
  84.3 1.5 fusion.5
  85.8 21.8 %collective-permute-done.5 = f32[1792,128]{1,0:T(8,128)} collective-permute-done((f32[1792,128]{1,0:T(8,128)}, f32[1792,128]{1,0:T(8,128)}, u32[]{:S(2)}, u32[]{:S(2)}) %collective-permute-start.5) | collective-permute-done | bytes 917536 | tf_op jit(solution)/shard_map/ppermute | solution.py:241
  108.8 1.5 fusion.7
  111.3 1.9 %collective-permute-start.7 = (f32[128,128]{1,0:T(8,128)S(1)}, f32[128,128]{1,0:T(8,128)S(1)}, u32[]{:S(2)}, u32[]{:S(2)}) collective-permute-start(f32[128,128]{1,0:T(8,128)S(1)} %fusion.3), channel_id=1, source_target_pairs={{0,1},{1,0},{2,3},{3,2},{4,5},{5,4},{6,7},{7,6},{8,9},{9,8},{10,11... | collective-permute-start | bytes 196616 | tf_op jit(solution)/shard_map/ppermute | solution.py:215
  114.5 11.3 %all_to_all.10 = f32[4,128,128]{2,1,0:T(8,128)S(1)} all-to-all(f32[4,128,128]{2,1,0:T(8,128)S(1)} %broadcast_in_dim.5), channel_id=1, replica_groups={{0,4,8,12},{1,5,9,13},{2,6,10,14},{3,7,11,15},{16,20,24,28},{17,21,25,2..., dimensions={0} | all-to-all | bytes 524288 | tf_op jit(solution)/shard_map/all_to_all | solution.py:222
  125.8 2.2 %collective-permute-start.8 = (f32[128,128]{1,0:T(8,128)S(1)}, f32[128,128]{1,0:T(8,128)S(1)}, u32[]{:S(2)}, u32[]{:S(2)}) collective-permute-start(f32[128,128]{1,0:T(8,128)S(1)} %fusion.15), channel_id=1, source_target_pairs={{0,2},{1,3},{2,0},{3,1},{4,6},{5,7},{6,4},{7,5},{8,10},{9,11},{10,... | collective-permute-start | bytes 196616 | tf_op jit(solution)/shard_map/ppermute | solution.py:215
  128.8 7.0 %collective-permute-done.8 = f32[128,128]{1,0:T(8,128)S(1)} collective-permute-done((f32[128,128]{1,0:T(8,128)S(1)}, f32[128,128]{1,0:T(8,128)S(1)}, u32[]{:S(2)}, u32[]{:S(2)}) %collective-permute-start.8) | collective-permute-done | bytes 65568 | tf_op jit(solution)/shard_map/ppermute | solution.py:215
  135.9 17.0 %eigen_steps.3 = (f32[256,256]{1,0:T(8,128)S(1)}, f32[256,256]{1,0:T(8,128)}) custom-call(f32[128,128]{1,0:T(8,128)S(1)} %get-tuple-element.23.lead_ref, f32[128,128]{1,0:T(8,128)S(1)} %add_multiply_fusion.cross_ref, f32[128,128]{1,0:T(8,128)S(1)} %get-tuple-element.22.trail_ref), custom_call_target="tpu_custom_call" | custom-call | tf_op jit(solution)/shard_map/eigen_steps/pallas_call | solution.py:199
  153.9 2.3 %convolution_add_fusion = f32[2048,256]{1,0:T(8,128)} fusion(f32[2048,256]{1,0:T(8,128)S(1)} %fusion.2, f32[2048,128]{1,0:T(8,128)S(1)} %convolution_bitcast_fusion.2, f32[1408,128]{1,0:T(8,128)S(1)} %slice.133, f32[640,128]{1,0:T(8,128)S(1)} %fusion.7, pred[]{:T(512)S(6)} %eq.11, f32[256,256]{1,0:T(8,128)S(1)} %get-tuple-element.20), kind=kOutput, calls=%fused_computation | convolution fusion | flops 403701760 | bytes 6422529 | tf_op jit(solution)/shard_map/dot_general | solution.py:247
  (31 shorter events, 11.9 us)
Async XLA Ops:
  0.6 12.2 %copy-start = (f32[2048,256]{1,0:T(8,128)S(1)}, f32[2048,256]{1,0:T(8,128)}, u32[]{:S(2)}) copy-start(f32[2048,256]{1,0:T(8,128)} %param.1) | copy-start | bytes 6291460
  4.9 3.2 %collective-permute-start = (f32[192,128]{1,0:T(8,128)S(1)}, f32[192,128]{1,0:T(8,128)S(1)}, u32[]{:S(2)}, u32[]{:S(2)}) collective-permute-start(f32[192,128]{1,0:T(8,128)S(1)} %slice_select_fusion.1), channel_id=1, source_target_pairs={{0,1},{1,0},{2,3},{3,2},{4,5},{5,4},{6,7},{7,6},{8,9},{9,8},{10,11... | collective-permute-start | bytes 294920 | tf_op jit(solution)/shard_map/ppermute | solution.py:215
  8.1 12.8 %collective-permute-start.1 = (f32[192,128]{1,0:T(8,128)S(1)}, f32[192,128]{1,0:T(8,128)S(1)}, u32[]{:S(2)}, u32[]{:S(2)}) collective-permute-start(f32[192,128]{1,0:T(8,128)S(1)} %select_add_fusion), channel_id=1, source_target_pairs={{0,2},{1,3},{2,0},{3,1},{4,6},{5,7},{6,4},{7,5},{8,10},{9,11},{10,... | collective-permute-start | bytes 294920 | tf_op jit(solution)/shard_map/ppermute | solution.py:215
  21.7 12.3 %all-to-all-start = ((f32[4,192,128]{2,1,0:T(8,128)}), f32[4,192,128]{2,1,0:T(8,128)S(1)}, u32[]{:S(2)}, u32[]{:S(2)}) async-start(f32[4,192,128]{2,1,0:T(8,128)} %broadcast_in_dim.4), calls=%async_computation | async-start | bytes 786432 | tf_op jit(solution)/shard_map/all_to_all | solution.py:222
  26.0 27.6 %collective-permute-start.4 = (f32[640,256]{1,0:T(8,128)S(1)}, f32[640,256]{1,0:T(8,128)}, u32[]{:S(2)}, u32[]{:S(2)}) collective-permute-start(f32[640,256]{1,0:T(8,128)S(1)} %slice.97), channel_id=1, source_target_pairs={{16,0},{32,16},{48,32},{64,48},{80,64},{96,80},{112,96},{128,112},... | collective-permute-start | bytes 1966088 | tf_op jit(solution)/shard_map/ppermute | solution.py:241
  29.9 30.1 %collective-permute-start.3 = (f32[640,256]{1,0:T(8,128)S(1)}, f32[640,256]{1,0:T(8,128)}, u32[]{:S(2)}, u32[]{:S(2)}) collective-permute-start(f32[640,256]{1,0:T(8,128)S(1)} %slice.97), channel_id=1, source_target_pairs={{0,16},{16,32},{32,48},{48,64},{64,80},{80,96},{96,112},{112,128},... | collective-permute-start | bytes 1966088 | tf_op jit(solution)/shard_map/ppermute | solution.py:241
  34.0 3.2 %collective-permute-start.2 = (f32[192,128]{1,0:T(8,128)S(1)}, f32[192,128]{1,0:T(8,128)S(1)}, u32[]{:S(2)}, u32[]{:S(2)}) collective-permute-start(f32[192,128]{1,0:T(8,128)S(1)} %fusion.13), channel_id=1, source_target_pairs={{0,1},{1,0},{2,3},{3,2},{4,5},{5,4},{6,7},{7,6},{8,9},{9,8},{10,11... | collective-permute-start | bytes 294920 | tf_op jit(solution)/shard_map/ppermute | solution.py:215
  61.7 22.5 %collective-permute-start.6 = (f32[1792,128]{1,0:T(8,128)}, f32[1792,128]{1,0:T(8,128)S(1)}, u32[]{:S(2)}, u32[]{:S(2)}) collective-permute-start(f32[1792,128]{1,0:T(8,128)} %pad_maximum_fusion.1), channel_id=1, source_target_pairs={{16,0},{32,16},{48,32},{64,48},{80,64},{96,80},{112,96},{128,112},... | collective-permute-start | bytes 2752520 | tf_op jit(solution)/shard_map/ppermute | solution.py:241
  66.0 41.6 %collective-permute-start.5 = (f32[1792,128]{1,0:T(8,128)}, f32[1792,128]{1,0:T(8,128)}, u32[]{:S(2)}, u32[]{:S(2)}) collective-permute-start(f32[1792,128]{1,0:T(8,128)} %pad_maximum_fusion), channel_id=1, source_target_pairs={{0,16},{16,32},{32,48},{48,64},{64,80},{80,96},{96,112},{112,128},... | collective-permute-start | bytes 2752520 | tf_op jit(solution)/shard_map/ppermute | solution.py:241
  111.3 3.1 %collective-permute-start.7 = (f32[128,128]{1,0:T(8,128)S(1)}, f32[128,128]{1,0:T(8,128)S(1)}, u32[]{:S(2)}, u32[]{:S(2)}) collective-permute-start(f32[128,128]{1,0:T(8,128)S(1)} %fusion.3), channel_id=1, source_target_pairs={{0,1},{1,0},{2,3},{3,2},{4,5},{5,4},{6,7},{7,6},{8,9},{9,8},{10,11... | collective-permute-start | bytes 196616 | tf_op jit(solution)/shard_map/ppermute | solution.py:215
  125.8 10.1 %collective-permute-start.8 = (f32[128,128]{1,0:T(8,128)S(1)}, f32[128,128]{1,0:T(8,128)S(1)}, u32[]{:S(2)}, u32[]{:S(2)}) collective-permute-start(f32[128,128]{1,0:T(8,128)S(1)} %fusion.15), channel_id=1, source_target_pairs={{0,2},{1,3},{2,0},{3,1},{4,6},{5,7},{6,4},{7,5},{8,10},{9,11},{10,... | collective-permute-start | bytes 196616 | tf_op jit(solution)/shard_map/ppermute | solution.py:215

commit v4 on v3

--- a/solution.py
+++ b/solution.py
@@ -14,7 +14,9 @@
 SQUARE = 2
 TURN = 3
 AHEAD = 2
-EARLY = 5
+WHOLE = 58 * 1024 * 1024
+STEP = 512
+EARLY = 4
 
 highest = lax.Precision.HIGHEST
 
@@ -146,6 +148,7 @@
 
 NN = ((1,), (0,))
 NT = ((1,), (1,))
+TN = ((0,), (0,))
 
 
 def eigen_kernel(lead_ref, cross_ref, trail_ref, rotation_ref, gram_ref, g, turns, z):
@@ -215,12 +218,15 @@
     return lax.ppermute(x, "rows", [(i, i ^ bit) for i in range(lax.axis_size("rows"))])
 
 
-def summed_over_x(x):
+def summed_over(x, groups):
+    copies = jnp.broadcast_to(x[None], (len(groups[0]),) + x.shape)
+    got = lax.all_to_all(copies, "rows", 0, 0, axis_index_groups=groups)
+    return jnp.sum(got, 0)
+
+
+def along_x():
     size = lax.axis_size("rows")
-    groups = [[c + (size // 4) * j for j in range(4)] for c in range(size // 4)]
-    copies = jnp.broadcast_to(x[None], (4,) + x.shape)
-    got = lax.all_to_all(copies, "rows", 0, 0, axis_index_groups=groups)
-    return (got[0] + got[1]) + (got[2] + got[3])
+    return [[c + (size // 4) * j for j in range(4)] for c in range(size // 4)]
 
 
 def core_halves(x):
@@ -249,53 +255,188 @@
     )
 
 
+def gram_kernel(columns_ref, gram_ref):
+    @pl.when(pl.program_id(0) == 0)
+    def _():
+        gram_ref[...] = jnp.zeros_like(gram_ref)
+
+    split = parts(columns_ref[...], 2)
+    gram_ref[...] += product(split, split, TN)
+
+
+def local_gram(columns):
+    rows, width = columns.shape
+    return pl.pallas_call(
+        gram_kernel,
+        grid=(rows // STEP,),
+        out_shape=jax.ShapeDtypeStruct((width, width), jnp.float32),
+        in_specs=[pl.BlockSpec((STEP, width), lambda i: (i, 0))],
+        out_specs=pl.BlockSpec((width, width), lambda i: (0, 0)),
+        compiler_params=pltpu.CompilerParams(vmem_limit_bytes=WHOLE),
+        name="local_gram",
+    )(columns)
+
+
+def send_kernel(ends_ref, columns_ref, rotation_ref, gram_ref, ahead_ref, back_ref):
+    step = pl.program_id(0)
+    steps = pl.num_programs(0)
+    first = ends_ref[0] == 1
+    to_lead, to_trail = rotation_ref[:, :BLK], rotation_ref[:, BLK:]
+    ahead = jnp.where(first, to_trail, to_lead)
+
+    @pl.when(step < steps - 1)
+    def _():
+        both = parts(jnp.concatenate([ahead, to_trail], 1), 2)
+        turned = product(parts(columns_ref[...], 2), both, NN)
+        ahead_ref[...] = turned[:, :BLK]
+        back_ref[...] = turned[:, BLK:]
+
+    @pl.when(step == steps - 1)
+    def _():
+        trail_gram = gram_ref[BLK:, BLK:]
+        ahead_ref[: 2 * BLK, :] = ahead
+        ahead_ref[2 * BLK :, :] = jnp.where(first, trail_gram, gram_ref[:BLK, :BLK])
+        back_ref[: 2 * BLK, :] = to_trail
+        back_ref[2 * BLK :, :] = trail_gram
+
+
+def to_send(ends, matrix, rotation, gram, late):
+    step = 3 * BLK
+    steps = late // step
+    payload = jax.ShapeDtypeStruct((late + step, BLK), jnp.float32)
+    block = pl.BlockSpec((step, BLK), lambda i: (i, 0))
+    whole = pl.BlockSpec((2 * BLK, 2 * BLK), lambda i: (0, 0))
+    return pl.pallas_call(
+        send_kernel,
+        grid=(steps + 1,),
+        out_shape=(payload, payload),
+        in_specs=[
+            pl.BlockSpec(memory_space=pltpu.SMEM),
+            pl.BlockSpec((step, 2 * BLK), lambda i: (jnp.minimum(i, steps - 1), 0)),
+            whole,
+            whole,
+        ],
+        out_specs=(block, block),
+        compiler_params=pltpu.CompilerParams(vmem_limit_bytes=32 * 1024 * 1024),
+        name="to_send",
+    )(ends, matrix, rotation, gram)
+
+
+def arrive_kernel(
+    ends_ref, own_ref, left_ref, left_turn_ref, from_left_ref, right_ref, right_turn_ref,
+    from_right_ref, paired_ref, cross_ref,
+):
+    step = pl.program_id(0)
+    steps = pl.num_programs(0)
+
+    @pl.when(step == 0)
+    def _():
+        cross_ref[...] = jnp.zeros_like(cross_ref)
+
+    def place(left, right):
+        leading = jnp.where(ends_ref[0] == 1, own_ref[...], left)
+        trailing = jnp.where(ends_ref[1] == 1, own_ref[...], right)
+        paired_ref[:, :BLK] = leading
+        paired_ref[:, BLK:] = trailing
+        cross_ref[...] += product(parts(leading, 2), parts(trailing, 2), TN)
+
+    @pl.when(step < steps - 1)
+    def _():
+        place(left_ref[...], right_ref[...])
+
+    @pl.when(step == steps - 1)
+    def _():
+        place(
+            product(parts(from_left_ref[...], 2), parts(left_turn_ref[...], 2), NN),
+            product(parts(from_right_ref[...], 2), parts(right_turn_ref[...], 2), NN),
+        )
+
+
+def arrived_pair(ends, own, over_left, from_left, over_right, from_right):
+    rows = own.shape[0]
+    early = from_left.shape[0]
+    steps = rows // early
+    turn_at = (rows - early) // (2 * BLK)
+    over = pl.BlockSpec((early, BLK), lambda i: (jnp.minimum(i, steps - 2), 0))
+    turn = pl.BlockSpec((2 * BLK, BLK), lambda i: (turn_at, 0))
+    moved_columns = pl.BlockSpec((early, 2 * BLK), lambda i: (0, 0))
+    return pl.pallas_call(
+        arrive_kernel,
+        grid=(steps,),
+        out_shape=(
+            jax.ShapeDtypeStruct((rows, 2 * BLK), jnp.float32),
+            jax.ShapeDtypeStruct((BLK, BLK), jnp.float32),
+        ),
+        in_specs=[
+            pl.BlockSpec(memory_space=pltpu.SMEM),
+            pl.BlockSpec((early, BLK), lambda i: (i, 0)),
+            over, turn, moved_columns, over, turn, moved_columns,
+        ],
+        out_specs=(
+            pl.BlockSpec((early, 2 * BLK), lambda i: (i, 0)),
+            pl.BlockSpec((BLK, BLK), lambda i: (0, 0)),
+        ),
+        compiler_params=pltpu.CompilerParams(vmem_limit_bytes=32 * 1024 * 1024),
+        name="arrived_pair",
+    )(ends, own, over_left, over_left, from_left, over_right, over_right, from_right)
+
+
+def turn_kernel(columns_ref, rotation_ref, paired_ref):
+    rotation = parts(rotation_ref[...], 2)
+    paired_ref[...] = product(parts(columns_ref[...], 2), rotation, NN)
+
+
+def turned_pair(columns, rotation):
+    rows, width = columns.shape
+    block = pl.BlockSpec((STEP, width), lambda i: (i, 0))
+    return pl.pallas_call(
+        turn_kernel,
+        grid=(rows // STEP,),
+        out_shape=jax.ShapeDtypeStruct((rows, width), jnp.float32),
+        in_specs=[block, pl.BlockSpec((width, width), lambda i: (0, 0))],
+        out_specs=block,
+        compiler_params=pltpu.CompilerParams(vmem_limit_bytes=WHOLE),
+        name="turned_pair",
+    )(columns, rotation)
+
+
 def per_device(matrix):
     seat = lax.axis_index("pairs")
     first = seat == 0
     last = seat == lax.axis_size("pairs") - 1
+    ends = jnp.stack([first, last]).astype(jnp.int32)
     rows_all = matrix.shape[0] * lax.axis_size("rows")
-    early = matrix.shape[0] * EARLY // 16
-
-    local = big(matrix, matrix, ((0,), (0,)))
+    late = matrix.shape[0] - matrix.shape[0] // EARLY
+
+    local = local_gram(matrix)
     packed = jnp.concatenate([local[:BLK, :BLK], local[:BLK, BLK:], local[BLK:, BLK:]], 0)
     part, odd = core_halves(packed)
     part = part + swapped(part, 2)
 
-    part, columns = lax.optimization_barrier((part, matrix[:early]))
+    part, columns = lax.optimization_barrier((part, matrix[late:]))
     from_left = moved(columns, 1)
     from_right = moved(columns, -1)
 
-    packed = both_halves(summed_over_x(part), odd) / rows_all
+    packed = both_halves(summed_over(part, along_x()), odd) / rows_all
     rotation, gram = eigen_steps(packed[:BLK], packed[BLK : 2 * BLK], packed[2 * BLK :])
-
     rotation, gram, from_left, from_right = lax.optimization_barrier(
         (rotation, gram, from_left, from_right)
     )
-    to_lead, to_trail = rotation[:, :BLK], rotation[:, BLK:]
-    lead_gram, trail_gram = gram[:BLK, :BLK], gram[BLK:, BLK:]
-    ahead = jnp.where(first, to_trail, to_lead)
-    ahead_gram = jnp.where(first, trail_gram, lead_gram)
-    rest = matrix[early:]
-    over_left = moved(jnp.concatenate([ahead, ahead_gram, big(rest, ahead, ((1,), (0,)))], 0), 1)
-    over_right = moved(
-        jnp.concatenate([to_trail, trail_gram, big(rest, to_trail, ((1,), (0,)))], 0), -1
-    )
-    own = big(matrix, to_lead, ((1,), (0,)))
-    turned_left = big(from_left, over_left[: 2 * BLK], ((1,), (0,)))
-    turned_right = big(from_right, over_right[: 2 * BLK], ((1,), (0,)))
-    new_leading = jnp.where(first, own, jnp.concatenate([turned_left, over_left[3 * BLK :]], 0))
-    new_trailing = jnp.where(last, own, jnp.concatenate([turned_right, over_right[3 * BLK :]], 0))
-    new_lead_gram = jnp.where(first, lead_gram, over_left[2 * BLK : 3 * BLK])
-    new_trail_gram = jnp.where(last, lead_gram, over_right[2 * BLK : 3 * BLK])
-
-    cross = big(new_leading, new_trailing, ((0,), (0,)))
-    cross = cross + swapped(cross, 1)
-    cross = summed_over_x(cross)
+
+    ahead, back = to_send(ends, matrix, rotation, gram, late)
+    over_left = moved(ahead, 1)
+    over_right = moved(back, -1)
+    own = big(matrix, rotation[:, :BLK], ((1,), (0,)))
+    columns, cross = arrived_pair(ends, own, over_left, from_left, over_right, from_right)
+    lead_gram = gram[:BLK, :BLK]
+    at = late + 2 * BLK
+    new_lead_gram = jnp.where(first, lead_gram, over_left[at:])
+    new_trail_gram = jnp.where(last, lead_gram, over_right[at:])
+
+    cross = summed_over(cross + swapped(cross, 1), along_x())
     cross = (cross + swapped(cross, 2)) / rows_all
     rotation, gram = eigen_steps(new_lead_gram, cross, new_trail_gram)
-    paired = big(new_leading, rotation[:BLK], ((1,), (0,)))
-    paired = paired + big(new_trailing, rotation[BLK:], ((1,), (0,)))
-    return paired, gram
+    return turned_pair(columns, rotation), gram
 
 
 def solution(mesh):

time: 157 us -> 163 us (1.038)
  the two profiles are of different devices: /device:TPU:504 before, /device:TPU:232 now
where the time goes in v4:
time: 163 us; the launch traced here: 162 us
  waiting for transfers between devices  64.2 us (39%)
  Pallas kernels  46.5 us (29%)
  starting transfers between devices  28.4 us (17%)
  blocking collectives  11.1 us (7%)
  local copies, waits for them, and re-layouts  5.45 us (3%)
  other arithmetic  4.45 us (3%)
    ppermute x4, waiting for transfers between devices, moved(): lax.ppermute(x, 'pairs', [(i - distance, i) for i in range(count) if 0 <=...  44.2 us
    pallas_call x2, Pallas kernels, eigen_steps(): pl.pallas_call(eigen_kernel, out_shape=(full, full), in_specs=[vmem] * 3,...  33 us
    ppermute x5, waiting for transfers between devices, swapped(): lax.ppermute(x, 'rows', [(i, i ^ bit) for i in range(lax.axis_size('rows'...  19.1 us
    ppermute x4, starting transfers between devices, moved(): lax.ppermute(x, 'pairs', [(i - distance, i) for i in range(count) if 0 <=...  13.5 us
    all_to_all x1, blocking collectives, summed_over(): got = lax.all_to_all(copies, 'rows', 0, 0, axis_index_groups=groups)  11.1 us
    ppermute x5, starting transfers between devices, swapped(): lax.ppermute(x, 'rows', [(i, i ^ bit) for i in range(lax.axis_size('rows'...  10.6 us
    pallas_call x1, Pallas kernels, turned_pair(): pl.pallas_call(turn_kernel, grid=(rows // STEP,), out_shape=jax.ShapeDtyp...  4.54 us
    all_to_all x1, starting transfers between devices, summed_over(): got = lax.all_to_all(copies, 'rows', 0, 0, axis_index_groups=groups)  4.29 us
  transfers between devices with their start and end apart: 10, of which 8 were waited for; matrix products, arithmetic and copies ran while one was open for 3% of the time, Pallas kernels for 10%

profile of v4, /device:TPU:232, one launch (start us, length us, event | category | flops | bytes accessed | tf_op | source)
XLA Modules:
  0.0 162.0 jit_solution(859564365823420115)
XLA Ops:
  0.6 4.3 %local_gram.1 = f32[256,256]{1,0:T(8,128)} custom-call(f32[2048,256]{1,0:T(8,128)} %columns_ref.3), custom_call_target="tpu_custom_call" | custom-call | tf_op jit(solution)/shard_map/local_gram/pallas_call | solution.py:269
  7.6 1.9 %collective-permute-start = (f32[192,128]{1,0:T(8,128)S(1)}, f32[192,128]{1,0:T(8,128)S(1)}, u32[]{:S(2)}, u32[]{:S(2)}) collective-permute-start(f32[192,128]{1,0:T(8,128)S(1)} %slice_select_fusion), channel_id=1, source_target_pairs={{0,1},{1,0},{2,3},{3,2},{4,5},{5,4},{6,7},{7,6},{8,9},{9,8},{10,11... | collective-permute-start | bytes 294920 | tf_op jit(solution)/shard_map/ppermute | solution.py:218
  9.5 1.3 collective-permute-done
  11.7 2.9 %collective-permute-start.1 = (f32[192,128]{1,0:T(8,128)S(1)}, f32[192,128]{1,0:T(8,128)S(1)}, u32[]{:S(2)}, u32[]{:S(2)}) collective-permute-start(f32[192,128]{1,0:T(8,128)S(1)} %select_add_fusion), channel_id=1, source_target_pairs={{0,2},{1,3},{2,0},{3,1},{4,6},{5,7},{6,4},{7,5},{8,10},{9,11},{10,... | collective-permute-start | bytes 294920 | tf_op jit(solution)/shard_map/ppermute | solution.py:218
  15.5 7.2 %collective-permute-done.1 = f32[192,128]{1,0:T(8,128)S(1)} collective-permute-done((f32[192,128]{1,0:T(8,128)S(1)}, f32[192,128]{1,0:T(8,128)S(1)}, u32[]{:S(2)}, u32[]{:S(2)}) %collective-permute-start.1) | collective-permute-done | bytes 98336 | tf_op jit(solution)/shard_map/ppermute | solution.py:218
  23.5 4.3 %all-to-all-start = ((f32[4,192,128]{2,1,0:T(8,128)}), f32[4,192,128]{2,1,0:T(8,128)S(1)}, u32[]{:S(2)}, u32[]{:S(2)}) async-start(f32[4,192,128]{2,1,0:T(8,128)} %broadcast_in_dim.4), calls=%async_computation | async-start | bytes 786432 | tf_op jit(solution)/shard_map/all_to_all | solution.py:223
  27.8 5.0 %collective-permute-start.4 = (f32[512,256]{1,0:T(8,128)}, f32[512,256]{1,0:T(8,128)S(1)}, u32[]{:S(2)}, u32[]{:S(2)}) collective-permute-start(f32[512,256]{1,0:T(8,128)} %slice.46), channel_id=1, source_target_pairs={{16,0},{32,16},{48,32},{64,48},{80,64},{96,80},{112,96},{128,112},... | collective-permute-start | bytes 1572872 | tf_op jit(solution)/shard_map/ppermute | solution.py:247
  32.8 1.9 %collective-permute-start.3 = (f32[512,256]{1,0:T(8,128)}, f32[512,256]{1,0:T(8,128)S(1)}, u32[]{:S(2)}, u32[]{:S(2)}) collective-permute-start(f32[512,256]{1,0:T(8,128)} %slice.46), channel_id=1, source_target_pairs={{0,16},{16,32},{32,48},{48,64},{64,80},{80,96},{96,112},{112,128},... | collective-permute-start | bytes 1572872 | tf_op jit(solution)/shard_map/ppermute | solution.py:247
  36.3 1.9 %collective-permute-start.2 = (f32[192,128]{1,0:T(8,128)}, f32[192,128]{1,0:T(8,128)S(1)}, u32[]{:S(2)}, u32[]{:S(2)}) collective-permute-start(f32[192,128]{1,0:T(8,128)} %reduce_sum.18), channel_id=1, source_target_pairs={{0,1},{1,0},{2,3},{3,2},{4,5},{5,4},{6,7},{7,6},{8,9},{9,8},{10,11... | collective-permute-start | bytes 294920 | tf_op jit(solution)/shard_map/ppermute | solution.py:218
  38.3 1.4 collective-permute-done.2
  40.7 16.2 %eigen_steps.2 = (f32[256,256]{1,0:T(8,128)S(1)}, f32[256,256]{1,0:T(8,128)S(1)}) custom-call(f32[128,128]{1,0:T(8,128)S(1)} %get-tuple-element.34.lead_ref, f32[128,128]{1,0:T(8,128)S(1)} %get-tuple-element.33.cross_ref, f32[128,128]{1,0:T(8,128)S(1)} %get-tuple-element.32.trail_ref), custom_call_target="tpu_custom_call" | custom-call | tf_op jit(solution)/shard_map/eigen_steps/pallas_call | solution.py:202
  57.0 2.1 %to_send.1 = (f32[1920,128]{1,0:T(8,128)S(1)}, f32[1920,128]{1,0:T(8,128)S(1)}) custom-call(s32[2]{0:T(128)S(1)} %add_convert_fusion.ends_ref, f32[2048,256]{1,0:T(8,128)S(1)} %copy-done, f32[256,256]{1,0:T(8,128)S(1)} %get-tuple-element.20.rotation_ref, f32[256,256]{1,0:T(8,128)S(1)} %get-tuple-element.21.gram_ref), custom_call_target="tpu_custom_call" | custom-call | tf_op jit(solution)/shard_map/to_send/pallas_call | solution.py:309
  59.1 3.9 %collective-permute-start.5 = (f32[1920,128]{1,0:T(8,128)S(1)}, f32[1920,128]{1,0:T(8,128)S(1)}, u32[]{:S(2)}, u32[]{:S(2)}) collective-permute-start(f32[1920,128]{1,0:T(8,128)S(1)} %get-tuple-element.22), channel_id=1, source_target_pairs={{0,16},{16,32},{32,48},{48,64},{64,80},{80,96},{96,112},{112,128},... | collective-permute-start | bytes 2949128 | tf_op jit(solution)/shard_map/ppermute | solution.py:247
  63.0 2.7 %collective-permute-start.6 = (f32[1920,128]{1,0:T(8,128)S(1)}, f32[1920,128]{1,0:T(8,128)S(1)}, u32[]{:S(2)}, u32[]{:S(2)}) collective-permute-start(f32[1920,128]{1,0:T(8,128)S(1)} %get-tuple-element.24), channel_id=1, source_target_pairs={{16,0},{32,16},{48,32},{64,48},{80,64},{96,80},{112,96},{128,112},... | collective-permute-start | bytes 2949128 | tf_op jit(solution)/shard_map/ppermute | solution.py:247
  66.8 19.6 %collective-permute-done.5.left_ref.left_turn_ref = f32[1920,128]{1,0:T(8,128)S(1)} collective-permute-done((f32[1920,128]{1,0:T(8,128)S(1)}, f32[1920,128]{1,0:T(8,128)S(1)}, u32[]{:S(2)}, u32[]{:S(2)}) %collective-permute-start.5) | collective-permute-done | bytes 983072 | tf_op jit(solution)/shard_map/ppermute | solution.py:247
  86.3 24.6 %collective-permute-done.6.right_ref.right_turn_ref = f32[1920,128]{1,0:T(8,128)S(1)} collective-permute-done((f32[1920,128]{1,0:T(8,128)S(1)}, f32[1920,128]{1,0:T(8,128)S(1)}, u32[]{:S(2)}, u32[]{:S(2)}) %collective-permute-start.6) | collective-permute-done | bytes 983072 | tf_op jit(solution)/shard_map/ppermute | solution.py:247
  111.0 2.6 %arrived_pair.1 = (f32[2048,256]{1,0:T(8,128)S(1)}, f32[128,128]{1,0:T(8,128)S(1)}) custom-call(s32[2]{0:T(128)S(1)} %add_convert_fusion.ends_ref, f32[2048,128]{1,0:T(8,128)S(1)} %convolution_bitcast_fusion.own_ref, f32[1920,128]{1,0:T(8,128)S(1)} %collective-permute-done.5.left_ref.left_turn_ref, ...), custom_call_target="tpu_custom_call" | custom-call | tf_op jit(solution)/shard_map/arrived_pair/pallas_call | solution.py:363
  113.6 1.3 copy-done.2
  114.9 1.9 %collective-permute-start.7 = (f32[128,128]{1,0:T(8,128)S(1)}, f32[128,128]{1,0:T(8,128)S(1)}, u32[]{:S(2)}, u32[]{:S(2)}) collective-permute-start(f32[128,128]{1,0:T(8,128)S(1)} %get-tuple-element.27), channel_id=1, source_target_pairs={{0,1},{1,0},{2,3},{3,2},{4,5},{5,4},{6,7},{7,6},{8,9},{9,8},{10,11... | collective-permute-start | bytes 196616 | tf_op jit(solution)/shard_map/ppermute | solution.py:218
  118.1 11.1 %all_to_all.10 = f32[4,128,128]{2,1,0:T(8,128)S(1)} all-to-all(f32[4,128,128]{2,1,0:T(8,128)S(1)} %broadcast_in_dim.5), channel_id=1, replica_groups={{0,4,8,12},{1,5,9,13},{2,6,10,14},{3,7,11,15},{16,20,24,28},{17,21,25,2..., dimensions={0} | all-to-all | bytes 524288 | tf_op jit(solution)/shard_map/all_to_all | solution.py:223
  129.2 1.9 %collective-permute-start.8 = (f32[128,128]{1,0:T(8,128)S(1)}, f32[128,128]{1,0:T(8,128)S(1)}, u32[]{:S(2)}, u32[]{:S(2)}) collective-permute-start(f32[128,128]{1,0:T(8,128)S(1)} %reduce_sum.19), channel_id=1, source_target_pairs={{0,2},{1,3},{2,0},{3,1},{4,6},{5,7},{6,4},{7,5},{8,10},{9,11},{10,... | collective-permute-start | bytes 196616 | tf_op jit(solution)/shard_map/ppermute | solution.py:218
  132.0 8.0 %collective-permute-done.8 = f32[128,128]{1,0:T(8,128)S(1)} collective-permute-done((f32[128,128]{1,0:T(8,128)S(1)}, f32[128,128]{1,0:T(8,128)S(1)}, u32[]{:S(2)}, u32[]{:S(2)}) %collective-permute-start.8) | collective-permute-done | bytes 65568 | tf_op jit(solution)/shard_map/ppermute | solution.py:218
  140.0 16.8 %eigen_steps.3 = (f32[256,256]{1,0:T(8,128)S(1)}, f32[256,256]{1,0:T(8,128)}) custom-call(f32[128,128]{1,0:T(8,128)S(1)} %get-tuple-element.31.lead_ref, f32[128,128]{1,0:T(8,128)S(1)} %add_multiply_fusion.cross_ref, f32[128,128]{1,0:T(8,128)S(1)} %get-tuple-element.30.trail_ref), custom_call_target="tpu_custom_call" | custom-call | tf_op jit(solution)/shard_map/eigen_steps/pallas_call | solution.py:202
  157.5 4.5 %turned_pair.1 = f32[2048,256]{1,0:T(8,128)} custom-call(f32[2048,256]{1,0:T(8,128)} %copy-done.2, f32[256,256]{1,0:T(8,128)} %copy-done.7), custom_call_target="tpu_custom_call" | custom-call | tf_op jit(solution)/shard_map/turned_pair/pallas_call | solution.py:392
  (36 shorter events, 11.7 us)
Async XLA Ops:
  0.6 14.0 %copy-start = (f32[2048,256]{1,0:T(8,128)S(1)}, f32[2048,256]{1,0:T(8,128)}, u32[]{:S(2)}) copy-start(f32[2048,256]{1,0:T(8,128)} %columns_ref.3) | copy-start | bytes 6291460
  7.6 3.2 %collective-permute-start = (f32[192,128]{1,0:T(8,128)S(1)}, f32[192,128]{1,0:T(8,128)S(1)}, u32[]{:S(2)}, u32[]{:S(2)}) collective-permute-start(f32[192,128]{1,0:T(8,128)S(1)} %slice_select_fusion), channel_id=1, source_target_pairs={{0,1},{1,0},{2,3},{3,2},{4,5},{5,4},{6,7},{7,6},{8,9},{9,8},{10,11... | collective-permute-start | bytes 294920 | tf_op jit(solution)/shard_map/ppermute | solution.py:218
  11.7 11.0 %collective-permute-start.1 = (f32[192,128]{1,0:T(8,128)S(1)}, f32[192,128]{1,0:T(8,128)S(1)}, u32[]{:S(2)}, u32[]{:S(2)}) collective-permute-start(f32[192,128]{1,0:T(8,128)S(1)} %select_add_fusion), channel_id=1, source_target_pairs={{0,2},{1,3},{2,0},{3,1},{4,6},{5,7},{6,4},{7,5},{8,10},{9,11},{10,... | collective-permute-start | bytes 294920 | tf_op jit(solution)/shard_map/ppermute | solution.py:218
  23.5 12.2 %all-to-all-start = ((f32[4,192,128]{2,1,0:T(8,128)}), f32[4,192,128]{2,1,0:T(8,128)S(1)}, u32[]{:S(2)}, u32[]{:S(2)}) async-start(f32[4,192,128]{2,1,0:T(8,128)} %broadcast_in_dim.4), calls=%async_computation | async-start | bytes 786432 | tf_op jit(solution)/shard_map/all_to_all | solution.py:223
  27.8 29.2 %collective-permute-start.4 = (f32[512,256]{1,0:T(8,128)}, f32[512,256]{1,0:T(8,128)S(1)}, u32[]{:S(2)}, u32[]{:S(2)}) collective-permute-start(f32[512,256]{1,0:T(8,128)} %slice.46), channel_id=1, source_target_pairs={{16,0},{32,16},{48,32},{64,48},{80,64},{96,80},{112,96},{128,112},... | collective-permute-start | bytes 1572872 | tf_op jit(solution)/shard_map/ppermute | solution.py:247
  32.8 24.2 %collective-permute-start.3 = (f32[512,256]{1,0:T(8,128)}, f32[512,256]{1,0:T(8,128)S(1)}, u32[]{:S(2)}, u32[]{:S(2)}) collective-permute-start(f32[512,256]{1,0:T(8,128)} %slice.46), channel_id=1, source_target_pairs={{0,16},{16,32},{32,48},{48,64},{64,80},{80,96},{96,112},{112,128},... | collective-permute-start | bytes 1572872 | tf_op jit(solution)/shard_map/ppermute | solution.py:247
  36.3 3.4 %collective-permute-start.2 = (f32[192,128]{1,0:T(8,128)}, f32[192,128]{1,0:T(8,128)S(1)}, u32[]{:S(2)}, u32[]{:S(2)}) collective-permute-start(f32[192,128]{1,0:T(8,128)} %reduce_sum.18), channel_id=1, source_target_pairs={{0,1},{1,0},{2,3},{3,2},{4,5},{5,4},{6,7},{7,6},{8,9},{9,8},{10,11... | collective-permute-start | bytes 294920 | tf_op jit(solution)/shard_map/ppermute | solution.py:218
  57.0 2.1 %copy-start.3 = (f32[512,256]{1,0:T(8,128)}, f32[512,256]{1,0:T(8,128)S(1)}, u32[]{:S(2)}) copy-start(f32[512,256]{1,0:T(8,128)S(1)} %collective-permute-done.4.from_right_ref) | copy-start | bytes 1572868
  57.0 2.1 %copy-start.5 = (f32[512,256]{1,0:T(8,128)}, f32[512,256]{1,0:T(8,128)S(1)}, u32[]{:S(2)}) copy-start(f32[512,256]{1,0:T(8,128)S(1)} %collective-permute-done.3.from_left_ref) | copy-start | bytes 1572868
  59.1 51.9 %copy-start.4 = (f32[512,256]{1,0:T(8,128)S(1)}, f32[512,256]{1,0:T(8,128)}, u32[]{:S(2)}) copy-start(f32[512,256]{1,0:T(8,128)} %copy-done.3) | copy-start | bytes 1572868
  59.1 51.9 %copy-start.6 = (f32[512,256]{1,0:T(8,128)S(1)}, f32[512,256]{1,0:T(8,128)}, u32[]{:S(2)}) copy-start(f32[512,256]{1,0:T(8,128)} %copy-done.5) | copy-start | bytes 1572868
  59.1 27.2 %collective-permute-start.5 = (f32[1920,128]{1,0:T(8,128)S(1)}, f32[1920,128]{1,0:T(8,128)S(1)}, u32[]{:S(2)}, u32[]{:S(2)}) collective-permute-start(f32[1920,128]{1,0:T(8,128)S(1)} %get-tuple-element.22), channel_id=1, source_target_pairs={{0,16},{16,32},{32,48},{48,64},{64,80},{80,96},{96,112},{112,128},... | collective-permute-start | bytes 2949128 | tf_op jit(solution)/shard_map/ppermute | solution.py:247
  63.0 48.0 %collective-permute-start.6 = (f32[1920,128]{1,0:T(8,128)S(1)}, f32[1920,128]{1,0:T(8,128)S(1)}, u32[]{:S(2)}, u32[]{:S(2)}) collective-permute-start(f32[1920,128]{1,0:T(8,128)S(1)} %get-tuple-element.24), channel_id=1, source_target_pairs={{16,0},{32,16},{48,32},{64,48},{80,64},{96,80},{112,96},{128,112},... | collective-permute-start | bytes 2949128 | tf_op jit(solution)/shard_map/ppermute | solution.py:247
  111.0 2.6 %copy-start.1 = (f32[1920,128]{1,0:T(8,128)}, f32[1920,128]{1,0:T(8,128)S(1)}, u32[]{:S(2)}) copy-start(f32[1920,128]{1,0:T(8,128)S(1)} %collective-permute-done.6.right_ref.right_turn_ref) | copy-start | bytes 2949124
  113.6 1.3 copy-start.2
  114.9 3.1 %collective-permute-start.7 = (f32[128,128]{1,0:T(8,128)S(1)}, f32[128,128]{1,0:T(8,128)S(1)}, u32[]{:S(2)}, u32[]{:S(2)}) collective-permute-start(f32[128,128]{1,0:T(8,128)S(1)} %get-tuple-element.27), channel_id=1, source_target_pairs={{0,1},{1,0},{2,3},{3,2},{4,5},{5,4},{6,7},{7,6},{8,9},{9,8},{10,11... | collective-permute-start | bytes 196616 | tf_op jit(solution)/shard_map/ppermute | solution.py:218
  129.2 10.8 %collective-permute-start.8 = (f32[128,128]{1,0:T(8,128)S(1)}, f32[128,128]{1,0:T(8,128)S(1)}, u32[]{:S(2)}, u32[]{:S(2)}) collective-permute-start(f32[128,128]{1,0:T(8,128)S(1)} %reduce_sum.19), channel_id=1, source_target_pairs={{0,2},{1,3},{2,0},{3,1},{4,6},{5,7},{6,4},{7,5},{8,10},{9,11},{10,... | collective-permute-start | bytes 196616 | tf_op jit(solution)/shard_map/ppermute | solution.py:218
  156.8 0.7 copy-start.7

commit v5 on v4

--- a/solution.py
+++ b/solution.py
@@ -14,7 +14,6 @@
 SQUARE = 2
 TURN = 3
 AHEAD = 2
-WHOLE = 58 * 1024 * 1024
 STEP = 512
 EARLY = 4
 
@@ -272,7 +271,7 @@
         out_shape=jax.ShapeDtypeStruct((width, width), jnp.float32),
         in_specs=[pl.BlockSpec((STEP, width), lambda i: (i, 0))],
         out_specs=pl.BlockSpec((width, width), lambda i: (0, 0)),
-        compiler_params=pltpu.CompilerParams(vmem_limit_bytes=WHOLE),
+        compiler_params=pltpu.CompilerParams(vmem_limit_bytes=32 * 1024 * 1024),
         name="local_gram",
     )(columns)
 
@@ -381,25 +380,6 @@
     )(ends, own, over_left, over_left, from_left, over_right, over_right, from_right)
 
 
-def turn_kernel(columns_ref, rotation_ref, paired_ref):
-    rotation = parts(rotation_ref[...], 2)
-    paired_ref[...] = product(parts(columns_ref[...], 2), rotation, NN)
-
-
-def turned_pair(columns, rotation):
-    rows, width = columns.shape
-    block = pl.BlockSpec((STEP, width), lambda i: (i, 0))
-    return pl.pallas_call(
-        turn_kernel,
-        grid=(rows // STEP,),
-        out_shape=jax.ShapeDtypeStruct((rows, width), jnp.float32),
-        in_specs=[block, pl.BlockSpec((width, width), lambda i: (0, 0))],
-        out_specs=block,
-        compiler_params=pltpu.CompilerParams(vmem_limit_bytes=WHOLE),
-        name="turned_pair",
-    )(columns, rotation)
-
-
 def per_device(matrix):
     seat = lax.axis_index("pairs")
     first = seat == 0
@@ -436,7 +416,7 @@
     cross = summed_over(cross + swapped(cross, 1), along_x())
     cross = (cross + swapped(cross, 2)) / rows_all
     rotation, gram = eigen_steps(new_lead_gram, cross, new_trail_gram)
-    return turned_pair(columns, rotation), gram
+    return big(columns, rotation, ((1,), (0,))), gram
 
 
 def solution(mesh):

time: 163 us -> 157 us (0.963)
  Pallas kernels: 46.5 us -> 39.4 us
  matrix products: 1 us -> 4.9 us
  other arithmetic: 4.45 us -> 2.67 us
    pallas_call x1 -> x0, Pallas kernels: 4.54 us -> none  [turned_pair(): pl.pallas_call(turn_kernel, grid=(rows // STEP,), out_shape=jax.ShapeDtyp...]
    dot_general x1 -> x2, matrix products: 1 us -> 4.9 us  [big(): lax.dot_general(a, b, (dims, ((), ())), precision=lax.Precision.HIGH, pre...]
    pallas_call x1, Pallas kernels: 4.28 us -> 1.74 us  [local_gram(): pl.pallas_call(gram_kernel, grid=(rows // STEP,), out_shape=jax.ShapeDtyp...]
where the time goes in v5:
time: 157 us; the launch traced here: 156 us
  waiting for transfers between devices  64.3 us (41%)
  Pallas kernels  39.4 us (25%)
  starting transfers between devices  28.4 us (18%)
  blocking collectives  11.1 us (7%)
  matrix products  4.9 us (3%)
  local copies, waits for them, and re-layouts  4.6 us (3%)
  other arithmetic  2.67 us (2%)
    ppermute x4, waiting for transfers between devices, moved(): lax.ppermute(x, 'pairs', [(i - distance, i) for i in range(count) if 0 <=...  44.3 us
    pallas_call x2, Pallas kernels, eigen_steps(): pl.pallas_call(eigen_kernel, out_shape=(full, full), in_specs=[vmem] * 3,...  33 us
    ppermute x5, waiting for transfers between devices, swapped(): lax.ppermute(x, 'rows', [(i, i ^ bit) for i in range(lax.axis_size('rows'...  19.1 us
    ppermute x4, starting transfers between devices, moved(): lax.ppermute(x, 'pairs', [(i - distance, i) for i in range(count) if 0 <=...  13.5 us
    all_to_all x1, blocking collectives, summed_over(): got = lax.all_to_all(copies, 'rows', 0, 0, axis_index_groups=groups)  11.1 us
    ppermute x5, starting transfers between devices, swapped(): lax.ppermute(x, 'rows', [(i, i ^ bit) for i in range(lax.axis_size('rows'...  10.6 us
    dot_general x2, matrix products, big(): lax.dot_general(a, b, (dims, ((), ())), precision=lax.Precision.HIGH, pre...  4.9 us
    all_to_all x1, starting transfers between devices, summed_over(): got = lax.all_to_all(copies, 'rows', 0, 0, axis_index_groups=groups)  4.3 us
  transfers between devices with their start and end apart: 10, of which 8 were waited for; matrix products, arithmetic and copies ran while one was open for 3% of the time, Pallas kernels for 10%

profile of v5, /device:TPU:232, one launch (start us, length us, event | category | flops | bytes accessed | tf_op | source)
XLA Modules:
  0.0 156.2 jit_solution(14419337155724369352)
XLA Ops:
  0.6 1.6 %copy-done = f32[2048,256]{1,0:T(8,128)S(1)} copy-done((f32[2048,256]{1,0:T(8,128)S(1)}, f32[2048,256]{1,0:T(8,128)}, u32[]{:S(2)}) %copy-start) | copy-done | bytes 2097176
  2.2 1.7 %local_gram.1 = f32[256,256]{1,0:T(8,128)S(1)} custom-call(f32[2048,256]{1,0:T(8,128)S(1)} %copy-done), custom_call_target="tpu_custom_call" | custom-call | tf_op jit(solution)/shard_map/local_gram/pallas_call | solution.py:268
  4.0 1.9 %collective-permute-start = (f32[192,128]{1,0:T(8,128)S(1)}, f32[192,128]{1,0:T(8,128)S(1)}, u32[]{:S(2)}, u32[]{:S(2)}) collective-permute-start(f32[192,128]{1,0:T(8,128)S(1)} %slice_select_fusion), channel_id=1, source_target_pairs={{0,1},{1,0},{2,3},{3,2},{4,5},{5,4},{6,7},{7,6},{8,9},{9,8},{10,11... | collective-permute-start | bytes 294920 | tf_op jit(solution)/shard_map/ppermute | solution.py:217
  7.3 2.9 %collective-permute-start.1 = (f32[192,128]{1,0:T(8,128)S(1)}, f32[192,128]{1,0:T(8,128)S(1)}, u32[]{:S(2)}, u32[]{:S(2)}) collective-permute-start(f32[192,128]{1,0:T(8,128)S(1)} %select_add_fusion), channel_id=1, source_target_pairs={{0,2},{1,3},{2,0},{3,1},{4,6},{5,7},{6,4},{7,5},{8,10},{9,11},{10,... | collective-permute-start | bytes 294920 | tf_op jit(solution)/shard_map/ppermute | solution.py:217
  11.0 7.2 %collective-permute-done.1 = f32[192,128]{1,0:T(8,128)S(1)} collective-permute-done((f32[192,128]{1,0:T(8,128)S(1)}, f32[192,128]{1,0:T(8,128)S(1)}, u32[]{:S(2)}, u32[]{:S(2)}) %collective-permute-start.1) | collective-permute-done | bytes 98336 | tf_op jit(solution)/shard_map/ppermute | solution.py:217
  19.0 4.3 %all-to-all-start = ((f32[4,192,128]{2,1,0:T(8,128)}), f32[4,192,128]{2,1,0:T(8,128)S(1)}, u32[]{:S(2)}, u32[]{:S(2)}) async-start(f32[4,192,128]{2,1,0:T(8,128)} %broadcast_in_dim.4), calls=%async_computation | async-start | bytes 786432 | tf_op jit(solution)/shard_map/all_to_all | solution.py:222
  23.3 5.0 %collective-permute-start.4 = (f32[512,256]{1,0:T(8,128)}, f32[512,256]{1,0:T(8,128)S(1)}, u32[]{:S(2)}, u32[]{:S(2)}) collective-permute-start(f32[512,256]{1,0:T(8,128)} %slice.46), channel_id=1, source_target_pairs={{16,0},{32,16},{48,32},{64,48},{80,64},{96,80},{112,96},{128,112},... | collective-permute-start | bytes 1572872 | tf_op jit(solution)/shard_map/ppermute | solution.py:246
  28.3 1.9 %collective-permute-start.3 = (f32[512,256]{1,0:T(8,128)}, f32[512,256]{1,0:T(8,128)S(1)}, u32[]{:S(2)}, u32[]{:S(2)}) collective-permute-start(f32[512,256]{1,0:T(8,128)} %slice.46), channel_id=1, source_target_pairs={{0,16},{16,32},{32,48},{48,64},{64,80},{80,96},{96,112},{112,128},... | collective-permute-start | bytes 1572872 | tf_op jit(solution)/shard_map/ppermute | solution.py:246
  31.9 1.9 %collective-permute-start.2 = (f32[192,128]{1,0:T(8,128)}, f32[192,128]{1,0:T(8,128)S(1)}, u32[]{:S(2)}, u32[]{:S(2)}) collective-permute-start(f32[192,128]{1,0:T(8,128)} %reduce_sum.18), channel_id=1, source_target_pairs={{0,1},{1,0},{2,3},{3,2},{4,5},{5,4},{6,7},{7,6},{8,9},{9,8},{10,11... | collective-permute-start | bytes 294920 | tf_op jit(solution)/shard_map/ppermute | solution.py:217
  33.9 1.4 collective-permute-done.2
  36.3 16.2 %eigen_steps.2 = (f32[256,256]{1,0:T(8,128)S(1)}, f32[256,256]{1,0:T(8,128)S(1)}) custom-call(f32[128,128]{1,0:T(8,128)S(1)} %get-tuple-element.34.lead_ref, f32[128,128]{1,0:T(8,128)S(1)} %get-tuple-element.33.cross_ref, f32[128,128]{1,0:T(8,128)S(1)} %get-tuple-element.32.trail_ref), custom_call_target="tpu_custom_call" | custom-call | tf_op jit(solution)/shard_map/eigen_steps/pallas_call | solution.py:201
  52.5 2.1 %to_send.1 = (f32[1920,128]{1,0:T(8,128)S(1)}, f32[1920,128]{1,0:T(8,128)S(1)}) custom-call(s32[2]{0:T(128)S(1)} %add_convert_fusion.ends_ref, f32[2048,256]{1,0:T(8,128)S(1)} %copy-done.1, f32[256,256]{1,0:T(8,128)S(1)} %get-tuple-element.20.rotation_ref, f32[256,256]{1,0:T(8,128)S(1)} %get-tuple-element.21.gram_ref), custom_call_target="tpu_custom_call" | custom-call | tf_op jit(solution)/shard_map/to_send/pallas_call | solution.py:308
  54.7 3.9 %collective-permute-start.5 = (f32[1920,128]{1,0:T(8,128)S(1)}, f32[1920,128]{1,0:T(8,128)S(1)}, u32[]{:S(2)}, u32[]{:S(2)}) collective-permute-start(f32[1920,128]{1,0:T(8,128)S(1)} %get-tuple-element.22), channel_id=1, source_target_pairs={{0,16},{16,32},{32,48},{48,64},{64,80},{80,96},{96,112},{112,128},... | collective-permute-start | bytes 2949128 | tf_op jit(solution)/shard_map/ppermute | solution.py:246
  58.6 2.7 %collective-permute-start.6 = (f32[1920,128]{1,0:T(8,128)S(1)}, f32[1920,128]{1,0:T(8,128)S(1)}, u32[]{:S(2)}, u32[]{:S(2)}) collective-permute-start(f32[1920,128]{1,0:T(8,128)S(1)} %get-tuple-element.24), channel_id=1, source_target_pairs={{16,0},{32,16},{48,32},{64,48},{80,64},{96,80},{112,96},{128,112},... | collective-permute-start | bytes 2949128 | tf_op jit(solution)/shard_map/ppermute | solution.py:246
  62.3 19.6 %collective-permute-done.5.left_ref.left_turn_ref = f32[1920,128]{1,0:T(8,128)S(1)} collective-permute-done((f32[1920,128]{1,0:T(8,128)S(1)}, f32[1920,128]{1,0:T(8,128)S(1)}, u32[]{:S(2)}, u32[]{:S(2)}) %collective-permute-start.5) | collective-permute-done | bytes 983072 | tf_op jit(solution)/shard_map/ppermute | solution.py:246
  81.9 24.7 %collective-permute-done.6.right_ref.right_turn_ref = f32[1920,128]{1,0:T(8,128)S(1)} collective-permute-done((f32[1920,128]{1,0:T(8,128)S(1)}, f32[1920,128]{1,0:T(8,128)S(1)}, u32[]{:S(2)}, u32[]{:S(2)}) %collective-permute-start.6) | collective-permute-done | bytes 983072 | tf_op jit(solution)/shard_map/ppermute | solution.py:246
  106.6 2.6 %arrived_pair.1 = (f32[2048,256]{1,0:T(8,128)S(1)}, f32[128,128]{1,0:T(8,128)S(1)}) custom-call(s32[2]{0:T(128)S(1)} %add_convert_fusion.ends_ref, f32[2048,128]{1,0:T(8,128)S(1)} %convolution_bitcast_fusion.own_ref, f32[1920,128]{1,0:T(8,128)S(1)} %collective-permute-done.5.left_ref.left_turn_ref, ...), custom_call_target="tpu_custom_call" | custom-call | tf_op jit(solution)/shard_map/arrived_pair/pallas_call | solution.py:362
  109.2 1.3 copy-done.3
  110.5 1.9 %collective-permute-start.7 = (f32[128,128]{1,0:T(8,128)S(1)}, f32[128,128]{1,0:T(8,128)S(1)}, u32[]{:S(2)}, u32[]{:S(2)}) collective-permute-start(f32[128,128]{1,0:T(8,128)S(1)} %get-tuple-element.27), channel_id=1, source_target_pairs={{0,1},{1,0},{2,3},{3,2},{4,5},{5,4},{6,7},{7,6},{8,9},{9,8},{10,11... | collective-permute-start | bytes 196616 | tf_op jit(solution)/shard_map/ppermute | solution.py:217
  113.7 11.1 %all_to_all.10 = f32[4,128,128]{2,1,0:T(8,128)S(1)} all-to-all(f32[4,128,128]{2,1,0:T(8,128)S(1)} %broadcast_in_dim.5), channel_id=1, replica_groups={{0,4,8,12},{1,5,9,13},{2,6,10,14},{3,7,11,15},{16,20,24,28},{17,21,25,2..., dimensions={0} | all-to-all | bytes 524288 | tf_op jit(solution)/shard_map/all_to_all | solution.py:222
  124.8 1.9 %collective-permute-start.8 = (f32[128,128]{1,0:T(8,128)S(1)}, f32[128,128]{1,0:T(8,128)S(1)}, u32[]{:S(2)}, u32[]{:S(2)}) collective-permute-start(f32[128,128]{1,0:T(8,128)S(1)} %reduce_sum.19), channel_id=1, source_target_pairs={{0,2},{1,3},{2,0},{3,1},{4,6},{5,7},{6,4},{7,5},{8,10},{9,11},{10,... | collective-permute-start | bytes 196616 | tf_op jit(solution)/shard_map/ppermute | solution.py:217
  127.6 8.0 %collective-permute-done.8 = f32[128,128]{1,0:T(8,128)S(1)} collective-permute-done((f32[128,128]{1,0:T(8,128)S(1)}, f32[128,128]{1,0:T(8,128)S(1)}, u32[]{:S(2)}, u32[]{:S(2)}) %collective-permute-start.8) | collective-permute-done | bytes 65568 | tf_op jit(solution)/shard_map/ppermute | solution.py:217
  135.6 16.8 %eigen_steps.3 = (f32[256,256]{1,0:T(8,128)S(1)}, f32[256,256]{1,0:T(8,128)}) custom-call(f32[128,128]{1,0:T(8,128)S(1)} %get-tuple-element.31.lead_ref, f32[128,128]{1,0:T(8,128)S(1)} %add_multiply_fusion.cross_ref, f32[128,128]{1,0:T(8,128)S(1)} %get-tuple-element.30.trail_ref), custom_call_target="tpu_custom_call" | custom-call | tf_op jit(solution)/shard_map/eigen_steps/pallas_call | solution.py:201
  152.3 3.9 %fusion.3 = f32[2048,256]{1,0:T(8,128)} fusion(f32[2048,256]{1,0:T(8,128)} %copy-done.3, f32[256,256]{1,0:T(8,128)S(1)} %get-tuple-element.28), kind=kOutput, calls=%fused_computation.12 | convolution fusion | flops 805306368 | bytes 4456448 | tf_op jit(solution)/shard_map/dot_general | solution.py:252
  (36 shorter events, 8.8 us)
Async XLA Ops:
  0.6 1.6 %copy-start = (f32[2048,256]{1,0:T(8,128)S(1)}, f32[2048,256]{1,0:T(8,128)}, u32[]{:S(2)}) copy-start(f32[2048,256]{1,0:T(8,128)} %columns_ref.3) | copy-start | bytes 6291460
  2.2 8.0 %copy-start.1 = (f32[2048,256]{1,0:T(8,128)S(1)}, f32[2048,256]{1,0:T(8,128)}, u32[]{:S(2)}) copy-start(f32[2048,256]{1,0:T(8,128)} %columns_ref.3) | copy-start | bytes 6291460
  4.0 3.2 %collective-permute-start = (f32[192,128]{1,0:T(8,128)S(1)}, f32[192,128]{1,0:T(8,128)S(1)}, u32[]{:S(2)}, u32[]{:S(2)}) collective-permute-start(f32[192,128]{1,0:T(8,128)S(1)} %slice_select_fusion), channel_id=1, source_target_pairs={{0,1},{1,0},{2,3},{3,2},{4,5},{5,4},{6,7},{7,6},{8,9},{9,8},{10,11... | collective-permute-start | bytes 294920 | tf_op jit(solution)/shard_map/ppermute | solution.py:217
  7.3 11.0 %collective-permute-start.1 = (f32[192,128]{1,0:T(8,128)S(1)}, f32[192,128]{1,0:T(8,128)S(1)}, u32[]{:S(2)}, u32[]{:S(2)}) collective-permute-start(f32[192,128]{1,0:T(8,128)S(1)} %select_add_fusion), channel_id=1, source_target_pairs={{0,2},{1,3},{2,0},{3,1},{4,6},{5,7},{6,4},{7,5},{8,10},{9,11},{10,... | collective-permute-start | bytes 294920 | tf_op jit(solution)/shard_map/ppermute | solution.py:217
  19.0 12.2 %all-to-all-start = ((f32[4,192,128]{2,1,0:T(8,128)}), f32[4,192,128]{2,1,0:T(8,128)S(1)}, u32[]{:S(2)}, u32[]{:S(2)}) async-start(f32[4,192,128]{2,1,0:T(8,128)} %broadcast_in_dim.4), calls=%async_computation | async-start | bytes 786432 | tf_op jit(solution)/shard_map/all_to_all | solution.py:222
  23.3 29.2 %collective-permute-start.4 = (f32[512,256]{1,0:T(8,128)}, f32[512,256]{1,0:T(8,128)S(1)}, u32[]{:S(2)}, u32[]{:S(2)}) collective-permute-start(f32[512,256]{1,0:T(8,128)} %slice.46), channel_id=1, source_target_pairs={{16,0},{32,16},{48,32},{64,48},{80,64},{96,80},{112,96},{128,112},... | collective-permute-start | bytes 1572872 | tf_op jit(solution)/shard_map/ppermute | solution.py:246
  28.3 24.2 %collective-permute-start.3 = (f32[512,256]{1,0:T(8,128)}, f32[512,256]{1,0:T(8,128)S(1)}, u32[]{:S(2)}, u32[]{:S(2)}) collective-permute-start(f32[512,256]{1,0:T(8,128)} %slice.46), channel_id=1, source_target_pairs={{0,16},{16,32},{32,48},{48,64},{64,80},{80,96},{96,112},{112,128},... | collective-permute-start | bytes 1572872 | tf_op jit(solution)/shard_map/ppermute | solution.py:246
  31.9 3.4 %collective-permute-start.2 = (f32[192,128]{1,0:T(8,128)}, f32[192,128]{1,0:T(8,128)S(1)}, u32[]{:S(2)}, u32[]{:S(2)}) collective-permute-start(f32[192,128]{1,0:T(8,128)} %reduce_sum.18), channel_id=1, source_target_pairs={{0,1},{1,0},{2,3},{3,2},{4,5},{5,4},{6,7},{7,6},{8,9},{9,8},{10,11... | collective-permute-start | bytes 294920 | tf_op jit(solution)/shard_map/ppermute | solution.py:217
  52.5 2.1 %copy-start.4 = (f32[512,256]{1,0:T(8,128)}, f32[512,256]{1,0:T(8,128)S(1)}, u32[]{:S(2)}) copy-start(f32[512,256]{1,0:T(8,128)S(1)} %collective-permute-done.4.from_right_ref) | copy-start | bytes 1572868
  52.5 2.1 %copy-start.6 = (f32[512,256]{1,0:T(8,128)}, f32[512,256]{1,0:T(8,128)S(1)}, u32[]{:S(2)}) copy-start(f32[512,256]{1,0:T(8,128)S(1)} %collective-permute-done.3.from_left_ref) | copy-start | bytes 1572868
  54.7 51.9 %copy-start.5 = (f32[512,256]{1,0:T(8,128)S(1)}, f32[512,256]{1,0:T(8,128)}, u32[]{:S(2)}) copy-start(f32[512,256]{1,0:T(8,128)} %copy-done.4) | copy-start | bytes 1572868
  54.7 51.9 %copy-start.7 = (f32[512,256]{1,0:T(8,128)S(1)}, f32[512,256]{1,0:T(8,128)}, u32[]{:S(2)}) copy-start(f32[512,256]{1,0:T(8,128)} %copy-done.6) | copy-start | bytes 1572868
  54.7 27.2 %collective-permute-start.5 = (f32[1920,128]{1,0:T(8,128)S(1)}, f32[1920,128]{1,0:T(8,128)S(1)}, u32[]{:S(2)}, u32[]{:S(2)}) collective-permute-start(f32[1920,128]{1,0:T(8,128)S(1)} %get-tuple-element.22), channel_id=1, source_target_pairs={{0,16},{16,32},{32,48},{48,64},{64,80},{80,96},{96,112},{112,128},... | collective-permute-start | bytes 2949128 | tf_op jit(solution)/shard_map/ppermute | solution.py:246
  58.6 48.0 %collective-permute-start.6 = (f32[1920,128]{1,0:T(8,128)S(1)}, f32[1920,128]{1,0:T(8,128)S(1)}, u32[]{:S(2)}, u32[]{:S(2)}) collective-permute-start(f32[1920,128]{1,0:T(8,128)S(1)} %get-tuple-element.24), channel_id=1, source_target_pairs={{16,0},{32,16},{48,32},{64,48},{80,64},{96,80},{112,96},{128,112},... | collective-permute-start | bytes 2949128 | tf_op jit(solution)/shard_map/ppermute | solution.py:246
  106.5 2.6 %copy-start.2 = (f32[1920,128]{1,0:T(8,128)}, f32[1920,128]{1,0:T(8,128)S(1)}, u32[]{:S(2)}) copy-start(f32[1920,128]{1,0:T(8,128)S(1)} %collective-permute-done.6.right_ref.right_turn_ref) | copy-start | bytes 2949124
  109.1 1.3 copy-start.3
  110.5 3.1 %collective-permute-start.7 = (f32[128,128]{1,0:T(8,128)S(1)}, f32[128,128]{1,0:T(8,128)S(1)}, u32[]{:S(2)}, u32[]{:S(2)}) collective-permute-start(f32[128,128]{1,0:T(8,128)S(1)} %get-tuple-element.27), channel_id=1, source_target_pairs={{0,1},{1,0},{2,3},{3,2},{4,5},{5,4},{6,7},{7,6},{8,9},{9,8},{10,11... | collective-permute-start | bytes 196616 | tf_op jit(solution)/shard_map/ppermute | solution.py:217
  124.8 10.8 %collective-permute-start.8 = (f32[128,128]{1,0:T(8,128)S(1)}, f32[128,128]{1,0:T(8,128)S(1)}, u32[]{:S(2)}, u32[]{:S(2)}) collective-permute-start(f32[128,128]{1,0:T(8,128)S(1)} %reduce_sum.19), channel_id=1, source_target_pairs={{0,2},{1,3},{2,0},{3,1},{4,6},{5,7},{6,4},{7,5},{8,10},{9,11},{10,... | collective-permute-start | bytes 196616 | tf_op jit(solution)/shard_map/ppermute | solution.py:217
